TPU v7x, 256 devices: a whole 4x4x8 slice. The times are simulated.
256 devices in a mesh: bucket: 64 (over z, y_lo, x), span: 4 (over y_hi, core).
Axes of the slice: x: 4, y: 4 (y_hi: 2, y_lo: 2; y = y_hi * 2 + y_lo), z: 8, core: 2. Of those that a mesh axis runs over, the one named last changes fastest.
Arguments:
- left_emb: bfloat16 [400, 65536], P(None, 'bucket'), may hold values from -1.5 to 1.5
- right_emb: bfloat16 [400, 65536], P(None, 'bucket'), may hold values from -1.5 to 1.5
- relation_weight: float32 [400, 16], replicated, may hold values from -6 to 6
- left_index: int32 [64, 4, 1024], P('bucket', 'span'), may hold values from 0 to 1023
- right_index: int32 [64, 4, 1024], P('bucket', 'span'), may hold values from 0 to 1023
- relation_index: int32 [64, 4, 1024], P('bucket', 'span'), may hold values from 0 to 15
- edge_count: int32 [64, 4], P('bucket', 'span'), may hold values from 1 to 1024, 2048 in all within a row
- neg_index: int32 [64, 1000], P('bucket'), may hold values from 0 to 1023
Outputs:
- left_grad: float32 [400, 65536], P(None, ('bucket', 'span'))
- right_grad: float32 [400, 65536], P(None, ('bucket', 'span'))
- relation_grad: float32 [400, 16], replicated
Inputs may be any that keep to these rules, and one draw needn't show every extreme that they name: `edge_count`: the 4 counts of one bucket sum to 2048, and in every bucket one of them equals 1024.
All inputs are finite; a program needn't handle non-finite values. No bound on the sum of `edge_count` on one device may be relied on, other than what follows from the above.
Results may differ from a plain program's by a relative error of at most 0.0033.
Values may be sent and summed in bfloat16 or wider, within the bound.
A program may use at most 64 MiB of HBM per device.

v0:
```python
import jax
import jax.numpy as jnp
from jax import lax
from jax.sharding import PartitionSpec as P


def passed_along(block, axis, distance):
    devices = range(lax.axis_size(axis))
    route = [((i - distance) % len(devices), i) for i in devices]
    return lax.ppermute(block, axis, route)


def make_query(relation_cols, right_values, half_width):
    rot_real = relation_cols[:, :half_width]
    rot_imag = relation_cols[:, half_width:]
    right_real = right_values[:, :half_width]
    right_imag = right_values[:, half_width:]
    return jnp.concatenate(
        [
            rot_real * right_real + rot_imag * right_imag,
            rot_real * right_imag - rot_imag * right_real,
        ],
        1,
    )


def edge_gradients(
    left_part,
    right_part,
    relation_weight,
    negatives,
    left_cols,
    right_cols,
    relation_ids,
    weight_mask,
):
    width = left_part.shape[0]
    half_width = width // 2
    count_neg = negatives.shape[0]
    left_table = left_part.T
    right_table = right_part.T
    left_rows = jnp.take(left_table, left_cols, axis=0).astype(jnp.float32)
    right_values = jnp.take(right_table, right_cols, axis=0).astype(jnp.float32)
    relation_rows = jnp.take(relation_weight.T, relation_ids, axis=0)
    query_short = make_query(relation_rows, right_values, half_width).astype(jnp.bfloat16)
    query_values = query_short.astype(jnp.float32)
    positive = jnp.sum(left_rows * query_values, 1)
    pos_weight = -jax.nn.sigmoid(-positive) * weight_mask
    negative_rows = jnp.take(left_table, negatives, axis=0)
    scores = lax.dot_general(
        query_short, negative_rows, (((1,), (1,)), ((), ())), preferred_element_type=jnp.float32
    )
    neg_weight = (jax.nn.sigmoid(scores) / count_neg * weight_mask[:, None]).astype(jnp.bfloat16)
    neg_parts = jnp.dot(neg_weight, negative_rows, preferred_element_type=jnp.float32)
    neg_total = lax.dot_general(
        neg_weight, query_short, (((0,), (0,)), ((), ())), preferred_element_type=jnp.float32
    )
    query_grad = left_rows * pos_weight[:, None] + neg_parts
    grad_real = query_grad[:, :half_width]
    grad_imag = query_grad[:, half_width:]
    rot_real = relation_rows[:, :half_width]
    rot_imag = relation_rows[:, half_width:]
    right_real = right_values[:, :half_width]
    right_imag = right_values[:, half_width:]
    right_rows_grad = jnp.concatenate(
        [grad_real * rot_real - grad_imag * rot_imag, grad_real * rot_imag + grad_imag * rot_real],
        1,
    )
    rotation_grad = jnp.concatenate(
        [
            grad_real * right_real + grad_imag * right_imag,
            grad_real * right_imag - grad_imag * right_real,
        ],
        1,
    )
    left_rows_total = (
        jnp.zeros((left_part.shape[1], width), jnp.float32)
        .at[left_cols]
        .add(query_values * pos_weight[:, None])
    )
    left_total = left_rows_total.at[negatives].add(neg_total).T
    right_total = (
        jnp.zeros((right_part.shape[1], width), jnp.float32).at[right_cols].add(right_rows_grad).T
    )
    relation_count = relation_weight.shape[1]
    one_hot = (
        relation_ids[:, None] == jnp.arange(relation_count, dtype=jnp.int32)[None, :]
    ).astype(jnp.float32)
    relation_total = lax.dot_general(
        rotation_grad,
        one_hot,
        (((0,), (0,)), ((), ())),
        precision=lax.Precision.HIGHEST,
        preferred_element_type=jnp.float32,
    )
    return (left_total, right_total, relation_total)


def per_device(
    left_emb,
    right_emb,
    relation_weight,
    left_index,
    right_index,
    relation_index,
    edge_count,
    neg_index,
):
    arrived = passed_along(right_emb, "bucket", 1)
    slot_total = left_index.shape[2]
    left_cols = left_index[0, 0]
    right_cols = right_index[0, 0]
    relation_ids = relation_index[0, 0]
    weight_mask = (jnp.arange(slot_total, dtype=jnp.int32) < edge_count[0, 0]).astype(jnp.float32)
    left_total, right_total, relation_total = edge_gradients(
        left_emb,
        arrived,
        relation_weight,
        neg_index[0],
        left_cols,
        right_cols,
        relation_ids,
        weight_mask,
    )
    left_grad = lax.psum_scatter(left_total, "span", scatter_dimension=1, tiled=True)
    returned = passed_along(right_total, "bucket", -1)
    right_grad = lax.psum_scatter(returned, "span", scatter_dimension=1, tiled=True)
    relation_grad = lax.psum(relation_total, ("bucket", "span"))
    return (left_grad, right_grad, relation_grad)


def solution(mesh):
    in_specs = (
        P(None, "bucket"),
        P(None, "bucket"),
        P(),
        P("bucket", "span", None),
        P("bucket", "span", None),
        P("bucket", "span", None),
        P("bucket", "span"),
        P("bucket", None),
    )
    out_specs = (P(None, ("bucket", "span")), P(None, ("bucket", "span")), P())
    return jax.shard_map(
        per_device, mesh=mesh, in_specs=in_specs, out_specs=out_specs, check_vma=False
    )
```

profile of v0, /device:TPU:33, one launch (start us, length us, event | category | flops | bytes accessed | tf_op | source)
XLA Modules:
  0.0 212.1 jit_solution(15296155276227381283)
XLA Ops:
  7.2 1.3 collective-permute-start
  8.5 0.7 fusion.13
  9.2 0.7 compare_and_fusion
  9.9 0.7 compare_and_fusion.1
  10.6 0.7 compare_select_fusion.2
  11.3 0.7 compare_and_fusion.3
  12.0 3.5 %gather_fusion = f32[1024,400]{1,0:T(8,128)S(1)} fusion(f32[16,400]{1,0:T(8,128)S(1)} %bitcast.25, s32[1024]{0:T(1024)S(1)} %broadcast_clamp_fusion), kind=kCustom, calls=%fused_computation.2 | custom fusion | bytes 3280896 | tf_op jit(solution)/shard_map/jit(_take)/gather | solution.py:44
  15.5 1.7 copy.26
  17.8 4.0 %gather_fusion.3 = bf16[1024,400]{1,0:T(8,128)(2,1)S(1)} fusion(bf16[1024,400]{1,0:T(8,128)(2,1)S(1)} %bitcast.26, s32[1024]{0:T(1024)S(1)} %fusion.13), kind=kCustom, calls=%fused_computation.1.clone | custom fusion | bytes 1642496 | tf_op jit(solution)/shard_map/jit(_take)/gather | solution.py:42
  21.8 1.3 copy.30
  23.8 5.1 %gather_fusion.1 = bf16[1000,400]{1,0:T(8,128)(2,1)} fusion(bf16[1024,400]{1,0:T(8,128)(2,1)S(1)} %bitcast.27, s32[1024]{0:T(1024)S(1)} %pad_clamp_fusion), kind=kCustom, calls=%fused_computation.3 | custom fusion | bytes 1604000 | tf_op jit(solution)/shard_map/jit(_take)/gather | solution.py:49
  29.7 1.4 copy.27
  31.2 5.1 %gather_fusion.2 = bf16[1024,400]{1,0:T(8,128)(2,1)} fusion(bf16[1024,400]{1,0:T(8,128)(2,1)S(1)} %bitcast.29, s32[1024]{0:T(1024)S(1)} %fusion.12), kind=kCustom, calls=%fused_computation.clone | custom fusion | bytes 1642496 | tf_op jit(solution)/shard_map/jit(_take)/gather | solution.py:43
  36.2 1.4 copy.28
  38.3 0.8 copy-done.4
  39.9 2.3 %multiply_convert_fusion = bf16[1024,1000]{0,1:T(8,128)(2,1)S(1)} fusion(f32[1024]{0:T(1024)S(1)} %get-tuple-element.19, bf16[1000,400]{1,0:T(8,128)(2,1)S(1)} %copy-done.9, pred[1000]{0:T(1024)(128)(4,1)S(1)} %compare_and_fusion.2, bf16[1024,200]{0,1:T(8,128)(2,1)S(1)} %get-tuple-element.15, bf16[1024,200]{0,1:T(8,128)(2,1)S(1)} %get-tuple-element.14), kind=kOutput, calls=%fused_computation.7 | convolution fusion | flops 826358400 | bytes 3672296 | tf_op jit(solution)/shard_map/dot_general | solution.py:50
  42.2 2.6 %fusion.17 = f32[1000,400]{1,0:T(8,128)} fusion(bf16[1024,1000]{0,1:T(8,128)(2,1)S(1)} %multiply_convert_fusion, bf16[1024,200]{0,1:T(8,128)(2,1)S(1)} %get-tuple-element.15, bf16[1024,200]{0,1:T(8,128)(2,1)S(1)} %get-tuple-element.14), kind=kOutput, calls=%fused_computation.57 | convolution fusion | flops 820838400 | bytes 4467200 | tf_op jit(solution)/shard_map/dot_general | solution.py:55
  45.0 1.9 copy.31
  46.9 7.8 %scatter_custom_fusion = f32[1024,400]{1,0:T(8,128)S(1)} fusion(s32[1024]{0:T(1024)S(1)} %bitcast.41, f32[1024,400]{1,0:T(8,128)} %copy.31, f32[]{:T(128)} %constant.25.clone.1), kind=kCustom, calls=%fused_computation.20 | custom fusion | flops 409600 | bytes 1638912 | tf_op jit(solution)/shard_map/scatter-add | solution.py:79
  54.6 8.2 %scatter_fusion = f32[1024,400]{1,0:T(8,128)S(1)} fusion(f32[1024,400]{1,0:T(8,128)S(1)} %scatter_custom_fusion, s32[1000]{0:T(1024)S(1)} %bitcast.34, f32[1000,400]{1,0:T(8,128)} %fusion.17), kind=kCustom, calls=%fused_computation.5 | custom fusion | flops 400000 | bytes 4804000 | tf_op jit(solution)/shard_map/scatter-add | solution.py:81
  62.9 1.3 copy-done.1
  64.3 3.1 %fusion.1 = f32[1024,400]{0,1:T(8,128)S(1)} fusion(bf16[1024,1000]{0,1:T(8,128)(2,1)} %copy-done.15, f32[1024]{0:T(1024)S(1)} %get-tuple-element.18, bf16[1024,400]{0,1:T(8,128)(2,1)S(1)} %copy-done.7, pred[1024]{0:T(1024)(128)(4,1)S(1)} %compare_and_fusion, bf16[1000,400]{1,0:T(8,128)(2,1)} %gather_fusion.1, pred[1000]{0:T(1024)(128)(4,1)S(1)} %compare_and_fusion.2), kind=kOutput, calls=%fused_computation.12 | convolution fusion | flops 821238400 | bytes 5311720 | tf_op jit(solution)/shard_map/dot_general | solution.py:54
  67.5 1.7 multiply_add_fusion
  69.4 1.8 copy.33
  71.2 7.8 %scatter_custom_fusion.2 = f32[1024,400]{1,0:T(8,128)S(1)} fusion(s32[1024]{0:T(1024)S(1)} %bitcast.42, f32[1024,400]{1,0:T(8,128)} %copy.33, f32[]{:T(128)} %constant.25.clone.1), kind=kCustom, calls=%fused_computation.18 | custom fusion | flops 409600 | bytes 1638912 | tf_op jit(solution)/shard_map/scatter-add | solution.py:83
  79.0 1.7 copy.34
  80.7 3.2 %collective-permute-start.1 = (f32[400,1024]{1,0:T(8,128)}, f32[400,1024]{1,0:T(8,128)S(1)}, u32[]{:S(2)}, u32[]{:S(2)}) collective-permute-start(f32[400,1024]{1,0:T(8,128)} %copy.34), channel_id=1, source_target_pairs={{4,0},{8,4},{12,8},{16,12},{20,16},{24,20},{28,24},{32,28},{36,32}... | collective-permute-start | bytes 4915208 | tf_op jit(solution)/shard_map/ppermute | solution.py:10
  83.8 34.5 %collective-permute-done.1 = f32[400,1024]{1,0:T(8,128)S(1)} collective-permute-done((f32[400,1024]{1,0:T(8,128)}, f32[400,1024]{1,0:T(8,128)S(1)}, u32[]{:S(2)}, u32[]{:S(2)}) %collective-permute-start.1) | collective-permute-done | bytes 1638432 | tf_op jit(solution)/shard_map/ppermute | solution.py:10
  118.3 1.2 copy-done.8
  119.5 2.2 %fusion.2 = f32[400,16]{0,1:T(8,128)S(1)} fusion(f32[1024,200]{0,1:T(8,128)} %get-tuple-element.11, f32[1024,200]{0,1:T(8,128)S(1)} %get-tuple-element.10, s32[1024]{0:T(1024)S(1)} %bitcast.32), kind=kOutput, calls=%fused_computation.14 | convolution fusion | flops 79069184 | bytes 1668096 | tf_op jit(solution)/shard_map/dot_general | solution.py:89
  121.7 81.6 %psum.7 = f32[400,16]{0,1:T(8,128)} all-reduce(f32[400,16]{0,1:T(8,128)S(1)} %fusion.2), channel_id=1, replica_groups=mesh['bucket'=64,'span'=4] {'bucket','span'}, use_global_device_ids=true, to_apply=%region_6.8 | all-reduce | flops 6400 | bytes 51200 | tf_op jit(solution)/shard_map/psum | solution.py:128
  203.3 2.0 copy.35
  (51 shorter events, 3.3 us)
Async XLA Ops:
  7.2 4.8 %copy-start = (f32[400,16]{0,1:T(8,128)S(1)}, f32[400,16]{0,1:T(8,128)}, u32[]{:S(2)}) copy-start(f32[400,16]{0,1:T(8,128)} %param.12) | copy-start | bytes 76804
  7.2 196.1 %reduce-scatter.3.cloned.1.call-start = ((), (), s32[]{:S(2)}) async-start(), calls=%async_computation.2 | async-start | bytes 2621440 | tf_op jit(solution)/shard_map/reduce_scatter | solution.py:125
  7.2 22.5 %collective-permute-start = (bf16[400,1024]{1,0:T(8,128)(2,1)}, bf16[400,1024]{1,0:T(8,128)(2,1)}, u32[]{:S(2)}, u32[]{:S(2)}) collective-permute-start(bf16[400,1024]{1,0:T(8,128)(2,1)} %param.11), channel_id=1, source_target_pairs={{252,0},{0,4},{4,8},{8,12},{12,16},{16,20},{20,24},{24,28},{28,32}... | collective-permute-start | bytes 2457608 | tf_op jit(solution)/shard_map/ppermute | solution.py:10
  15.5 1.8 copy-start.10
  17.8 5.9 %copy-start.14 = (s32[1,1000]{1,0:T(1,128)S(1)}, s32[1,1000]{1,0:T(1,128)}, u32[]{:S(2)}) copy-start(s32[1,1000]{1,0:T(1,128)} %param.17) | copy-start | bytes 12004
  23.7 5.1 %copy-start.13 = (s32[1,1,1024]{2,1,0:T(1,128)S(1)}, s32[1,1,1024]{2,1,0:T(1,128)}, u32[]{:S(2)}) copy-start(s32[1,1,1024]{2,1,0:T(1,128)} %param.14) | copy-start | bytes 12292
  23.7 5.1 %copy-start.12 = (s32[1,1,1024]{2,1,0:T(1,128)S(1)}, s32[1,1,1024]{2,1,0:T(1,128)}, u32[]{:S(2)}) copy-start(s32[1,1,1024]{2,1,0:T(1,128)} %param.13) | copy-start | bytes 12292
  23.8 5.1 %copy-start.6 = (f32[1024,400]{0,1:T(8,128)S(1)}, f32[1024,400]{0,1:T(8,128)}, u32[]{:S(2)}) copy-start(f32[1024,400]{0,1:T(8,128)} %copy.26) | copy-start | bytes 4915204
  29.1 8.7 %copy-start.2 = (f32[1024,400]{0,1:T(8,128)}, f32[1024,400]{0,1:T(8,128)S(1)}, u32[]{:S(2)}) copy-start(f32[1024,400]{0,1:T(8,128)S(1)} %broadcast_select_fusion.1) | copy-start | bytes 4915204
  37.8 1.3 copy-start.4
  37.8 1.7 copy-start.7
  37.8 2.1 copy-start.9
  42.2 2.6 %copy-start.15 = (bf16[1024,1000]{0,1:T(8,128)(2,1)}, bf16[1024,1000]{0,1:T(8,128)(2,1)S(1)}, u32[]{:S(2)}) copy-start(bf16[1024,1000]{0,1:T(8,128)(2,1)S(1)} %multiply_convert_fusion) | copy-start | bytes 6144004
  62.8 1.4 copy-start.1
  64.2 141.0 %reduce-scatter.5.cloned.1.call-start = ((), (), s32[]{:S(2)}) async-start(), calls=%async_computation.3 | async-start | bytes 2048000 | tf_op jit(solution)/shard_map/reduce_scatter | solution.py:127
  64.3 3.2 %copy-start.3 = (f32[1024,400]{0,1:T(8,128)S(1)}, f32[1024,400]{0,1:T(8,128)}, u32[]{:S(2)}) copy-start(f32[1024,400]{0,1:T(8,128)} %copy-done.2) | copy-start | bytes 4915204
  64.3 3.2 %copy-start.5 = (f32[1024,400]{0,1:T(8,128)S(1)}, f32[1024,400]{0,1:T(8,128)}, u32[]{:S(2)}) copy-start(f32[1024,400]{0,1:T(8,128)} %copy-done.4) | copy-start | bytes 4915204
  79.0 40.6 %copy-start.11 = (s32[1,1,1024]{2,1,0:T(1,128)S(1)}, s32[1,1,1024]{2,1,0:T(1,128)}, u32[]{:S(2)}) copy-start(s32[1,1,1024]{2,1,0:T(1,128)} %param.15) | copy-start | bytes 12292
  80.7 37.6 %collective-permute-start.1 = (f32[400,1024]{1,0:T(8,128)}, f32[400,1024]{1,0:T(8,128)S(1)}, u32[]{:S(2)}, u32[]{:S(2)}) collective-permute-start(f32[400,1024]{1,0:T(8,128)} %copy.34), channel_id=1, source_target_pairs={{4,0},{8,4},{12,8},{16,12},{20,16},{24,20},{28,24},{32,28},{36,32}... | collective-permute-start | bytes 4915208 | tf_op jit(solution)/shard_map/ppermute | solution.py:10
  118.3 1.2 copy-start.8
Sparse Core Ops, SparseCore 0:
  64.3 45.9 reduce-scatter.2
  119.6 61.2 reduce-scatter.4
where the time goes:
time: 216 us; the launch traced here: 212 us
  blocking collectives  81.6 us (38%)
  local copies, waits for them, and re-layouts  35.3 us (16%)
  waiting for transfers between devices  35.1 us (16%)
  other arithmetic  30.4 us (14%)
  between operations  15 us (7%)
  matrix products  10.2 us (5%)
  starting transfers between devices  4.53 us (2%)
    psum x1, blocking collectives, per_device(): relation_grad = lax.psum(relation_total, ('bucket', 'span'))  81.6 us
    ppermute x2, waiting for transfers between devices, passed_along(): return lax.ppermute(block, axis, route)  35.1 us
    scatter-add x1, other arithmetic, edge_gradients(): left_total = left_rows_total.at[negatives].add(neg_total).T  8.22 us
    scatter-add x1, other arithmetic, edge_gradients(): left_rows_total = jnp.zeros((left_part.shape[1], width), jnp.float32).at[...  7.76 us
    scatter-add x1, other arithmetic, edge_gradients(): jnp.zeros((right_part.shape[1], width), jnp.float32).at[right_cols]  7.76 us
    gather x2, local copies, waits for them, and re-layouts, edge_gradients(): right_values = jnp.take(right_table, right_cols, axis=0).astype(jnp.float32)  6.49 us
    unnamed x34, local copies, waits for them, and re-layouts  6.39 us
    gather x2, local copies, waits for them, and re-layouts, edge_gradients(): relation_rows = jnp.take(relation_weight.T, relation_ids, axis=0)  5.25 us
  transfers between devices with their start and end apart: 4, of which 2 were waited for; matrix products, arithmetic and copies ran while one was open for 19% of the time, Pallas kernels for 0%

commit v1 on v0

v1 whole, which is shorter than its diff:
```python
import functools
import math

import jax
import jax.numpy as jnp
from jax import lax
from jax.experimental import pallas as pl
from jax.experimental.pallas import tpu as pltpu
from jax.sharding import PartitionSpec as P

MESH = pl.DeviceIdType.MESH
CHUNKS = 4
TILE = 256
F32 = jnp.float32
BF16 = jnp.bfloat16


def nt_dot(a, b):
    return lax.dot_general(a, b, (((1,), (1,)), ((), ())), preferred_element_type=F32)


def dot(a, b):
    return jnp.dot(a, b, preferred_element_type=F32)


def kernel(
    inner,
    left_hbm,
    right_hbm,
    relw_hbm,
    lidx_hbm,
    ridx_hbm,
    relidx_hbm,
    count_hbm,
    neg_hbm,
    left_out,
    right_out,
    rel_out,
    left,
    left_t,
    relw,
    wcat,
    own_idx,
    own_count,
    neg,
    cnt,
    idx_buf,
    edges,
    rbuf,
    query_s,
    w_tile,
    w_own,
    rrg_hi,
    rrg_lo,
    rel_acc,
    back_send,
    back_recv,
    left_stage,
    rb1,
    rb2,
    rb3,
    load_sem,
    idx_send,
    idx_recv,
    fwd_send,
    fwd_recv,
    pass_send,
    back_ssem,
    back_rsem,
    r1_send,
    r1_recv,
    r2_send,
    r2_recv,
    r3_send,
    r3_recv,
    out_sem,
):
    width, part = left.shape
    half = width // 2
    n_bucket = lax.axis_size("bucket")
    n_span = lax.axis_size("span")
    outer = n_bucket // inner
    b = lax.axis_index("bucket")
    s = lax.axis_index("span")
    count_neg = neg.shape[1]
    total_edges = edges.shape[1]
    slots = own_idx.shape[2]
    own_width = part // n_span
    chunk = part // CHUNKS
    core = lax.rem(s, 2)
    sibling = s + 1 - 2 * core
    nxt = lax.rem(b + 1, n_bucket)
    prv = lax.rem(b + n_bucket - 1, n_bucket)
    j = lax.rem(b, inner)
    zi = lax.div(b, inner)

    loads = [
        pltpu.make_async_copy(src, dst, load_sem.at[i])
        for i, (src, dst) in enumerate(
            [
                (lidx_hbm.at[0], own_idx.at[0]),
                (ridx_hbm.at[0], own_idx.at[1]),
                (relidx_hbm.at[0], own_idx.at[2]),
                (count_hbm, own_count),
                (neg_hbm, neg),
                (relw_hbm, relw),
                (left_hbm, left),
            ]
        )
    ]
    for load in loads:
        load.start()

    barrier = pltpu.get_barrier_semaphore()
    peers = [(nxt, s), (prv, s)]
    span_peers = [(b, lax.rem(s + d, n_span)) for d in range(1, n_span)]
    inner_peers = [(zi * inner + lax.rem(j + d, inner), s) for d in range(1, inner)]
    outer_peers = [(lax.rem(zi + d, outer) * inner + j, s) for d in range(1, outer)]
    peers = peers + span_peers + inner_peers + outer_peers
    for peer in peers:
        pl.semaphore_signal(barrier, inc=1, device_id=peer, device_id_type=MESH)
    pl.semaphore_wait(barrier, len(peers))

    fwd = []
    for i in range(CHUNKS // 2):
        k = core * (CHUNKS // 2) + i
        fwd.append(
            pltpu.make_async_remote_copy(
                src_ref=right_hbm.at[:, pl.ds(pl.multiple_of(k * chunk, chunk), chunk)],
                dst_ref=rbuf.at[k],
                send_sem=fwd_send.at[i],
                recv_sem=fwd_recv.at[k],
                device_id=(nxt, s),
                device_id_type=MESH,
            )
        )
        fwd[-1].start()

    for load in loads[:4]:
        load.wait()
    slot = lax.broadcasted_iota(jnp.int32, (1, slots), 1)
    live = slot < own_count[...]
    idx_buf[s, 0:1, :] = jnp.where(live, own_idx[0], -1)
    idx_buf[s, 1:2, :] = own_idx[1]
    idx_buf[s, 2:3, :] = own_idx[2]
    idx_buf[s, 3:4, :] = jnp.zeros((1, slots), jnp.int32)
    idx_copies = []
    for d, peer in enumerate(span_peers):
        idx_copies.append(
            pltpu.make_async_remote_copy(
                src_ref=idx_buf.at[s],
                dst_ref=idx_buf.at[s],
                send_sem=idx_send.at[d],
                recv_sem=idx_recv.at[s],
                device_id=peer,
                device_id_type=MESH,
            )
        )
        idx_copies[-1].start()

    loads[4].wait()
    for k in range(part // 128):
        col = lax.broadcasted_iota(jnp.int32, (128, count_neg), 0) + k * 128
        hits = jnp.where(col == neg[...], 1.0, 0.0).astype(F32)
        times = jnp.sum(hits, axis=1, keepdims=True) * (1.0 / count_neg)
        cnt[k * 128 : (k + 1) * 128, :] = jnp.broadcast_to(times, (128, 128))

    loads[5].wait()
    rel_count = relw.shape[1]
    w0 = relw[...]
    w_hi = w0.astype(BF16)
    w1 = w0 - w_hi.astype(F32)
    w_mid = w1.astype(BF16)
    w_lo = (w1 - w_mid.astype(F32)).astype(BF16)
    row = lax.broadcasted_iota(jnp.int32, (rel_count, 128), 0)
    lane = lax.broadcasted_iota(jnp.int32, (rel_count, 128), 1)
    placed = jnp.zeros((width, 128), F32)
    for t, term in enumerate((w_hi, w_mid, w_lo)):
        put = jnp.where(lane == row + t * rel_count, 1.0, 0.0).astype(BF16)
        placed = placed + dot(term, put)
    wcat[...] = placed.astype(BF16)

    loads[6].wait()
    for k in range(part // 128):
        block = left[:, k * 128 : (k + 1) * 128].astype(F32)
        left_t[k * 128 : (k + 1) * 128, :] = block.T.astype(BF16)

    for d in range(1, n_span):
        c = lax.rem(s + d, n_span)
        pltpu.make_async_remote_copy(
            src_ref=idx_buf.at[c],
            dst_ref=idx_buf.at[c],
            send_sem=idx_send.at[d - 1],
            recv_sem=idx_recv.at[c],
            device_id=(b, c),
            device_id_type=MESH,
        ).wait_recv()
    rank = lax.broadcasted_iota(jnp.int32, (4, total_edges), 1)
    packed = jnp.zeros((4, total_edges), jnp.int32)
    start = jnp.zeros((1, 1), jnp.int32)
    for c in range(n_span):
        value = idx_buf[c]
        alive = jnp.where(value[0:1, :] >= 0, 1.0, 0.0).astype(F32)
        size = jnp.sum(alive, axis=1, keepdims=True).astype(jnp.int32)
        value = jnp.concatenate([value, jnp.zeros((4, total_edges - slots), jnp.int32)], axis=1)
        if c > 0:
            for bit in range((total_edges - 1).bit_length()):
                moved = pltpu.roll(value, 1 << bit, 1)
                on = jnp.broadcast_to(start & (1 << bit), (4, total_edges)) != 0
                value = jnp.where(on, moved, value)
        inside = (rank >= start) & (rank < start + size)
        packed = jnp.where(inside, value, packed)
        start = start + size
    edges[...] = packed

    passes = []
    for i in range(CHUNKS // 2):
        k = core * (CHUNKS // 2) + i
        fwd[i].wait_recv()
        passes.append(
            pltpu.make_async_remote_copy(
                src_ref=rbuf.at[k],
                dst_ref=rbuf.at[k],
                send_sem=pass_send.at[i],
                recv_sem=fwd_recv.at[k],
                device_id=(b, sibling),
                device_id_type=MESH,
            )
        )
        passes[-1].start()
    for i in range(CHUNKS // 2):
        k = (1 - core) * (CHUNKS // 2) + i
        pltpu.make_async_remote_copy(
            src_ref=rbuf.at[k],
            dst_ref=rbuf.at[k],
            send_sem=pass_send.at[i],
            recv_sem=fwd_recv.at[k],
            device_id=(b, sibling),
            device_id_type=MESH,
        ).wait_recv()

    rel_acc[...] = jnp.zeros_like(rel_acc)
    own_start = pl.multiple_of(s * own_width, own_width)

    def tile_step(t, _):
        at = pl.ds(pl.multiple_of(t * TILE, TILE), TILE)
        l_row = edges[0:1, at]
        r_row = edges[1:2, at]
        t_row = edges[2:3, at]
        right_rows = jnp.zeros((width, TILE), F32)
        for k in range(CHUNKS):
            col = lax.broadcasted_iota(jnp.int32, (chunk, TILE), 0) + k * chunk
            pick = jnp.where(col == r_row, 1.0, 0.0).astype(BF16)
            right_rows = right_rows + dot(rbuf[k], pick)
        kind = lax.broadcasted_iota(jnp.int32, (128, TILE), 0)
        pick_rel = jnp.where((kind & (rel_count - 1)) == t_row, 1.0, 0.0).astype(BF16)
        rot = dot(wcat[...], pick_rel)
        w_re, w_im = rot[:half], rot[half:]
        r_re, r_im = right_rows[:half], right_rows[half:]
        query = jnp.concatenate(
            [w_re * r_re + w_im * r_im, w_re * r_im - w_im * r_re], axis=0
        ).astype(BF16)
        query_s[:, at] = query
        scores = dot(left_t[...], query)
        col = lax.broadcasted_iota(jnp.int32, (part, TILE), 0)
        is_left = col == l_row
        positive = jnp.sum(jnp.where(is_left, scores, 0.0), axis=0, keepdims=True)
        pos_weight = -1.0 / (1.0 + jnp.exp(positive))
        times = cnt[...]
        times = jnp.concatenate([times] * (TILE // 128), axis=1)
        weight = times / (1.0 + jnp.exp(-scores))
        weight = (weight + jnp.where(is_left, pos_weight, 0.0)).astype(BF16)
        w_tile[...] = weight
        w_own[:, at] = w_tile[pl.ds(own_start, own_width), :]
        grad = dot(left[...], weight)
        a, c = grad[:half], grad[half:]
        rows = jnp.concatenate([a * w_re - c * w_im, a * w_im + c * w_re], axis=0)
        hi = rows.astype(BF16)
        rrg_hi[:, at] = hi
        rrg_lo[:, at] = (rows - hi.astype(F32)).astype(BF16)
        turn = jnp.concatenate([a * r_re + c * r_im, a * r_im - c * r_re], axis=0).astype(BF16)
        own_kind = lax.broadcasted_iota(jnp.int32, (16, TILE), 0) + s * (rel_count // n_span)
        pick_own = jnp.where(own_kind == t_row, 1.0, 0.0).astype(BF16)
        rel_acc[...] += nt_dot(pick_own, turn)
        return 0

    lax.fori_loop(0, total_edges // TILE, tile_step, 0)

    def exchange(buf, me, peers, slots_of, send_sem, recv_sem):
        copies = []
        for d, (peer, other) in enumerate(zip(peers, slots_of)):
            copies.append(
                (
                    pltpu.make_async_remote_copy(
                        src_ref=buf.at[me],
                        dst_ref=buf.at[me],
                        send_sem=send_sem.at[d],
                        recv_sem=recv_sem.at[me],
                        device_id=peer,
                        device_id_type=MESH,
                    ),
                    pltpu.make_async_remote_copy(
                        src_ref=buf.at[other],
                        dst_ref=buf.at[other],
                        send_sem=send_sem.at[d],
                        recv_sem=recv_sem.at[other],
                        device_id=peer,
                        device_id_type=MESH,
                    ),
                )
            )
            copies[-1][0].start()
        return copies

    rel_rows = rel_count // n_span
    rb1[j] = rel_acc[0:rel_rows, :]
    stage1 = exchange(
        rb1, j, inner_peers, [lax.rem(j + d, inner) for d in range(1, inner)], r1_send, r1_recv
    )

    r_all = edges[1:2, :]
    col = lax.broadcasted_iota(jnp.int32, (own_width, total_edges), 0) + s * own_width
    pick = jnp.where(col == r_all, 1.0, 0.0).astype(BF16)
    right_own = nt_dot(rrg_hi[...], pick) + nt_dot(rrg_lo[...], pick)
    back_send[...] = right_own.astype(BF16)
    back = pltpu.make_async_remote_copy(
        src_ref=back_send,
        dst_ref=back_recv,
        send_sem=back_ssem,
        recv_sem=back_rsem,
        device_id=(prv, s),
        device_id_type=MESH,
    )
    back.start()

    for _, incoming in stage1:
        incoming.wait_recv()
    rb2[zi] = jnp.sum(rb1[...], axis=0)
    stage2 = exchange(
        rb2, zi, outer_peers, [lax.rem(zi + d, outer) for d in range(1, outer)], r2_send, r2_recv
    )

    left_stage[...] = nt_dot(query_s[...], w_own[...])
    left_copy = pltpu.make_async_copy(left_stage, left_out, out_sem.at[0])
    left_copy.start()

    for _, incoming in stage2:
        incoming.wait_recv()
    rb3[s] = jnp.sum(rb2[...], axis=0)
    stage3 = exchange(
        rb3, s, span_peers, [lax.rem(s + d, n_span) for d in range(1, n_span)], r3_send, r3_recv
    )
    for _, incoming in stage3:
        incoming.wait_recv()
    rel_copy = pltpu.make_async_copy(rb3, rel_out, out_sem.at[2])
    rel_copy.start()

    back.wait_recv()
    right_copy = pltpu.make_async_copy(back_recv, right_out, out_sem.at[1])
    right_copy.start()

    for copy in fwd + idx_copies + passes:
        copy.wait_send()
    back.wait_send()
    for stage in (stage1, stage2, stage3):
        for outgoing, _ in stage:
            outgoing.wait_send()
    left_copy.wait()
    rel_copy.wait()
    right_copy.wait()


def solution(mesh):
    n_bucket = mesh.shape["bucket"]
    n_span = mesh.shape["span"]
    inner = math.isqrt(n_bucket)
    outer = n_bucket // inner

    def per_device(
        left_emb,
        right_emb,
        relation_weight,
        left_index,
        right_index,
        relation_index,
        edge_count,
        neg_index,
    ):
        width, part = left_emb.shape
        slots = left_index.shape[2]
        total_edges = 2 * slots
        own = part // n_span
        rel_count = relation_weight.shape[1]
        rel_rows = rel_count // n_span
        any_space = pl.BlockSpec(memory_space=pl.ANY)
        dma = pltpu.SemaphoreType.DMA
        left_grad, right_grad, rel_grad = pl.pallas_call(
            functools.partial(kernel, inner),
            out_shape=(
                jax.ShapeDtypeStruct((width, own), F32),
                jax.ShapeDtypeStruct((width, own), BF16),
                jax.ShapeDtypeStruct((n_span, rel_rows, width), F32),
            ),
            in_specs=[any_space] * 8,
            out_specs=[any_space] * 3,
            scratch_shapes=[
                pltpu.VMEM((width, part), BF16),
                pltpu.VMEM((part, width), BF16),
                pltpu.VMEM((width, rel_count), F32),
                pltpu.VMEM((width, 128), BF16),
                pltpu.VMEM((3, 1, slots), jnp.int32),
                pltpu.VMEM((1, 1), jnp.int32),
                pltpu.VMEM((1, neg_index.shape[1]), jnp.int32),
                pltpu.VMEM((part, 128), F32),
                pltpu.VMEM((n_span, 4, slots), jnp.int32),
                pltpu.VMEM((4, total_edges), jnp.int32),
                pltpu.VMEM((CHUNKS, width, part // CHUNKS), BF16),
                pltpu.VMEM((width, total_edges), BF16),
                pltpu.VMEM((part, TILE), BF16),
                pltpu.VMEM((own, total_edges), BF16),
                pltpu.VMEM((width, total_edges), BF16),
                pltpu.VMEM((width, total_edges), BF16),
                pltpu.VMEM((16, width), F32),
                pltpu.VMEM((width, own), BF16),
                pltpu.VMEM((width, own), BF16),
                pltpu.VMEM((width, own), F32),
                pltpu.VMEM((inner, rel_rows, width), F32),
                pltpu.VMEM((outer, rel_rows, width), F32),
                pltpu.VMEM((n_span, rel_rows, width), F32),
                dma((7,)),
                dma((n_span - 1,)),
                dma((n_span,)),
                dma((CHUNKS // 2,)),
                dma((CHUNKS,)),
                dma((CHUNKS // 2,)),
                dma,
                dma,
                dma((inner,)),
                dma((inner,)),
                dma((outer,)),
                dma((outer,)),
                dma((n_span,)),
                dma((n_span,)),
                dma((3,)),
            ],
            compiler_params=pltpu.CompilerParams(
                collective_id=0, has_side_effects=True, vmem_limit_bytes=48 * 1024 * 1024
            ),
        )(
            left_emb,
            right_emb,
            relation_weight,
            left_index,
            right_index,
            relation_index,
            edge_count,
            neg_index,
        )
        rel_grad = rel_grad.reshape(rel_count, width).T
        return left_grad, right_grad.astype(F32), rel_grad

    in_specs = (
        P(None, "bucket"),
        P(None, "bucket"),
        P(),
        P("bucket", "span", None),
        P("bucket", "span", None),
        P("bucket", "span", None),
        P("bucket", "span"),
        P("bucket", None),
    )
    out_specs = (P(None, ("bucket", "span")), P(None, ("bucket", "span")), P())
    return jax.shard_map(
        per_device, mesh=mesh, in_specs=in_specs, out_specs=out_specs, check_vma=False
    )
```

time: 216 us -> 62.7 us (0.29); the launches traced: 212 us -> 62.5 us
  blocking collectives: 81.6 us -> 0 us
  Pallas kernels: 0 us -> 55.7 us
  waiting for transfers between devices: 35.1 us -> 0 us
  local copies, waits for them, and re-layouts: 35.3 us -> 4.58 us
  other arithmetic: 30.4 us -> 0.78 us
  between operations: 15 us -> 1.37 us
  matrix products: 10.2 us -> 0 us
  starting transfers between devices: 4.53 us -> 0 us
    psum x1 -> x0, blocking collectives: 81.6 us -> none  [per_device(): relation_grad = lax.psum(relation_total, ('bucket', 'span'))]
    pallas_call x0 -> x1, Pallas kernels: none -> 55.7 us  [per_device(): pl.pallas_call(functools.partial(kernel, inner), out_shape=(jax.ShapeDtyp...]
    ppermute x2 -> x0, waiting for transfers between devices: 35.1 us -> none  [passed_along(): return lax.ppermute(block, axis, route)]
    scatter-add x3 -> x0, other arithmetic: 23.7 us -> none  [the longest x1 8.22 us: edge_gradients(): left_total = left_rows_total.at[negatives].add(neg_total).T]
    gather x7 -> x0, local copies, waits for them, and re-layouts: 22.1 us -> none  [the longest x2 6.49 us: edge_gradients(): right_values = jnp.take(right_table, right_cols, axis=0).astype(jnp.float32)]
    dot_general x4 -> x0, matrix products: 10.2 us -> none  [the longest x1 3.13 us: edge_gradients(): jnp.dot(neg_weight, negative_rows, preferred_element_type=jnp.float32)]
    ppermute x2 -> x0, starting transfers between devices: 4.45 us -> none  [passed_along(): return lax.ppermute(block, axis, route)]
    unnamed x34 -> x14, local copies, waits for them, and re-layouts: 6.39 us -> 3.95 us
  transfers between devices with their start and end apart: 4 -> 0, of which waited for: 2 -> 0; matrix products, arithmetic and copies ran while one was open for 19% -> 0% of each run, Pallas kernels for 0% -> 0%
where the time goes in v1:
time: 62.7 us; the launch traced here: 62.5 us
  Pallas kernels  55.7 us (89%)
  local copies, waits for them, and re-layouts  4.58 us (7%)
  between operations  1.37 us (2%)
  other arithmetic  0.78 us (1%)
    pallas_call x1, Pallas kernels, per_device(): pl.pallas_call(functools.partial(kernel, inner), out_shape=(jax.ShapeDtyp...  55.7 us
    unnamed x14, local copies, waits for them, and re-layouts  3.95 us

profile of v1, /device:TPU:33, one launch (start us, length us, event | category | flops | bytes accessed | tf_op | source)
XLA Modules:
  0.0 62.5 jit_solution(9861041387847739615)
XLA Ops:
  1.3 0.0 copy-start.2
  1.3 0.0 copy-start.3
  1.3 0.0 copy-start.4
  1.3 0.0 copy-start.5
  1.3 0.9 %copy.11.relw_hbm = f32[400,16]{1,0:T(8,128)S(1)} copy(f32[400,16]{0,1:T(8,128)} %param.10) | data formatting | bytes 51200 | tf_op args[2]
  2.2 0.0 copy-done.2
  2.2 0.0 copy-done.3
  2.2 0.0 copy-done.4
  2.3 0.0 copy-done.5
  2.3 0.0 copy-start
  2.3 1.1 %copy-done = bf16[400,1024]{1,0:T(8,128)(2,1)S(1)} copy-done((bf16[400,1024]{1,0:T(8,128)(2,1)S(1)}, bf16[400,1024]{1,0:T(8,128)(2,1)}, u32[]{:S(2)}) %copy-start) | copy-done | bytes 819224
  3.4 0.0 copy-start.1
  3.4 1.1 %copy-done.1 = bf16[400,1024]{1,0:T(8,128)(2,1)S(1)} copy-done((bf16[400,1024]{1,0:T(8,128)(2,1)S(1)}, bf16[400,1024]{1,0:T(8,128)(2,1)}, u32[]{:S(2)}) %copy-start.1) | copy-done | bytes 819224
  4.6 55.7 %shard_map.103 = (f32[400,256]{1,0:T(8,128)S(1)}, bf16[400,256]{1,0:T(8,128)(2,1)S(1)}, f32[4,4,400]{2,1,0:T(4,128)S(1)}) custom-call(bf16[400,1024]{1,0:T(8,128)(2,1)S(1)} %copy-done, bf16[400,1024]{1,0:T(8,128)(2,1)S(1)} %copy-done.1, f32[400,16]{1,0:T(8,128)S(1)} %copy.11.relw_hbm, s32[1,1,1024]{2,1,0:T(1,128)S(1)} %copy-done.2, ...), custom_call_target="tpu_custom_call" | custom-call | tf_op jit(solution)/shard_map/pallas_call | solution.py:397
  60.3 0.6 %reshape.9 = f32[16,400]{1,0:T(8,128)} reshape(f32[4,4,400]{2,1,0:T(4,128)S(1)} %get-tuple-element.8) | data formatting | bytes 51200 | tf_op jit(solution)/shard_map/reshape | solution.py:459
  60.9 0.8 %convert_element_type.3 = f32[400,256]{1,0:T(8,128)} convert(bf16[400,256]{1,0:T(8,128)(2,1)S(1)} %get-tuple-element.7) | non-fusion elementwise | flops 102400 | bytes 614400 | tf_op jit(solution)/shard_map/convert_element_type | solution.py:460
  61.7 0.8 %copy.14 = f32[400,256]{1,0:T(8,128)} copy(f32[400,256]{1,0:T(8,128)S(1)} %get-tuple-element.12) | data formatting | bytes 819200
Async XLA Ops:
  1.3 1.0 %copy-start.2 = (s32[1,1,1024]{2,1,0:T(1,128)S(1)}, s32[1,1,1024]{2,1,0:T(1,128)}, u32[]{:S(2)}) copy-start(s32[1,1,1024]{2,1,0:T(1,128)} %lidx_hbm.1) | copy-start | bytes 12292
  1.3 1.0 %copy-start.3 = (s32[1,1,1024]{2,1,0:T(1,128)S(1)}, s32[1,1,1024]{2,1,0:T(1,128)}, u32[]{:S(2)}) copy-start(s32[1,1,1024]{2,1,0:T(1,128)} %ridx_hbm.1) | copy-start | bytes 12292
  1.3 1.0 %copy-start.4 = (s32[1,1,1024]{2,1,0:T(1,128)S(1)}, s32[1,1,1024]{2,1,0:T(1,128)}, u32[]{:S(2)}) copy-start(s32[1,1,1024]{2,1,0:T(1,128)} %relidx_hbm.1) | copy-start | bytes 12292
  1.3 1.0 %copy-start.5 = (s32[1,1000]{1,0:T(1,128)S(1)}, s32[1,1000]{1,0:T(1,128)}, u32[]{:S(2)}) copy-start(s32[1,1000]{1,0:T(1,128)} %neg_hbm.1) | copy-start | bytes 12004
  2.3 1.1 %copy-start = (bf16[400,1024]{1,0:T(8,128)(2,1)S(1)}, bf16[400,1024]{1,0:T(8,128)(2,1)}, u32[]{:S(2)}) copy-start(bf16[400,1024]{1,0:T(8,128)(2,1)} %left_hbm.1) | copy-start | bytes 2457604
  3.4 1.1 %copy-start.1 = (bf16[400,1024]{1,0:T(8,128)(2,1)S(1)}, bf16[400,1024]{1,0:T(8,128)(2,1)}, u32[]{:S(2)}) copy-start(bf16[400,1024]{1,0:T(8,128)(2,1)} %right_hbm.1) | copy-start | bytes 2457604

commit v2 on v1

--- a/solution.py
+++ b/solution.py
@@ -10,7 +10,7 @@
 
 MESH = pl.DeviceIdType.MESH
 CHUNKS = 4
-TILE = 256
+TILE = 512
 F32 = jnp.float32
 BF16 = jnp.bfloat16
 
@@ -48,14 +48,16 @@
     edges,
     rbuf,
     query_s,
-    w_tile,
-    w_own,
+    w_s,
     rrg_hi,
     rrg_lo,
     rel_acc,
     back_send,
-    back_recv,
     left_stage,
+    right_rows_s,
+    rel_part,
+    right_part,
+    left_part,
     rb1,
     rb2,
     rb3,
@@ -67,6 +69,8 @@
     pass_send,
     back_ssem,
     back_rsem,
+    part_send,
+    part_recv,
     r1_send,
     r1_recv,
     r2_send,
@@ -94,6 +98,14 @@
     j = lax.rem(b, inner)
     zi = lax.div(b, inner)
 
+    barrier = pltpu.get_barrier_semaphore()
+    peers = [(nxt, s), (prv, s)]
+    span_peers = [(b, lax.rem(s + d, n_span)) for d in range(1, n_span)]
+    inner_peers = [(zi * inner + lax.rem(j + d, inner), s) for d in range(1, inner)]
+    outer_peers = [(lax.rem(zi + d, outer) * inner + j, s) for d in range(1, outer)]
+    peers = peers + span_peers + inner_peers + outer_peers
+    for peer in peers:
+        pl.semaphore_signal(barrier, inc=1, device_id=peer, device_id_type=MESH)
     loads = [
         pltpu.make_async_copy(src, dst, load_sem.at[i])
         for i, (src, dst) in enumerate(
@@ -111,15 +123,30 @@
     for load in loads:
         load.start()
 
-    barrier = pltpu.get_barrier_semaphore()
-    peers = [(nxt, s), (prv, s)]
-    span_peers = [(b, lax.rem(s + d, n_span)) for d in range(1, n_span)]
-    inner_peers = [(zi * inner + lax.rem(j + d, inner), s) for d in range(1, inner)]
-    outer_peers = [(lax.rem(zi + d, outer) * inner + j, s) for d in range(1, outer)]
-    peers = peers + span_peers + inner_peers + outer_peers
-    for peer in peers:
-        pl.semaphore_signal(barrier, inc=1, device_id=peer, device_id_type=MESH)
+    for load in loads[:4]:
+        load.wait()
+    slot = lax.broadcasted_iota(jnp.int32, (1, slots), 1)
+    live = slot < own_count[...]
+    idx_buf[s, 0:1, :] = jnp.where(live, own_idx[0], -1)
+    idx_buf[s, 1:2, :] = own_idx[1]
+    idx_buf[s, 2:3, :] = own_idx[2]
+    idx_buf[s, 3:4, :] = jnp.zeros((1, slots), jnp.int32)
+
     pl.semaphore_wait(barrier, len(peers))
+
+    idx_copies = []
+    for d, peer in enumerate(span_peers):
+        idx_copies.append(
+            pltpu.make_async_remote_copy(
+                src_ref=idx_buf.at[s],
+                dst_ref=idx_buf.at[s],
+                send_sem=idx_send.at[d],
+                recv_sem=idx_recv.at[s],
+                device_id=peer,
+                device_id_type=MESH,
+            )
+        )
+        idx_copies[-1].start()
 
     fwd = []
     for i in range(CHUNKS // 2):
@@ -136,28 +163,6 @@
         )
         fwd[-1].start()
 
-    for load in loads[:4]:
-        load.wait()
-    slot = lax.broadcasted_iota(jnp.int32, (1, slots), 1)
-    live = slot < own_count[...]
-    idx_buf[s, 0:1, :] = jnp.where(live, own_idx[0], -1)
-    idx_buf[s, 1:2, :] = own_idx[1]
-    idx_buf[s, 2:3, :] = own_idx[2]
-    idx_buf[s, 3:4, :] = jnp.zeros((1, slots), jnp.int32)
-    idx_copies = []
-    for d, peer in enumerate(span_peers):
-        idx_copies.append(
-            pltpu.make_async_remote_copy(
-                src_ref=idx_buf.at[s],
-                dst_ref=idx_buf.at[s],
-                send_sem=idx_send.at[d],
-                recv_sem=idx_recv.at[s],
-                device_id=peer,
-                device_id_type=MESH,
-            )
-        )
-        idx_copies[-1].start()
-
     loads[4].wait()
     for k in range(part // 128):
         col = lax.broadcasted_iota(jnp.int32, (128, count_neg), 0) + k * 128
@@ -166,19 +171,13 @@
         cnt[k * 128 : (k + 1) * 128, :] = jnp.broadcast_to(times, (128, 128))
 
     loads[5].wait()
-    rel_count = relw.shape[1]
+    rel_count = relw.shape[0]
     w0 = relw[...]
-    w_hi = w0.astype(BF16)
-    w1 = w0 - w_hi.astype(F32)
-    w_mid = w1.astype(BF16)
-    w_lo = (w1 - w_mid.astype(F32)).astype(BF16)
-    row = lax.broadcasted_iota(jnp.int32, (rel_count, 128), 0)
-    lane = lax.broadcasted_iota(jnp.int32, (rel_count, 128), 1)
-    placed = jnp.zeros((width, 128), F32)
-    for t, term in enumerate((w_hi, w_mid, w_lo)):
-        put = jnp.where(lane == row + t * rel_count, 1.0, 0.0).astype(BF16)
-        placed = placed + dot(term, put)
-    wcat[...] = placed.astype(BF16)
+    w_hi = w0.astype(BF16).astype(F32)
+    w_mid = (w0 - w_hi).astype(BF16).astype(F32)
+    w_lo = w0 - w_hi - w_mid
+    blank = jnp.zeros((128 - 3 * rel_count, width), F32)
+    wcat[...] = jnp.concatenate([w_hi, w_mid, w_lo, blank], axis=0).T.astype(BF16)
 
     loads[6].wait()
     for k in range(part // 128):
@@ -213,6 +212,18 @@
         start = start + size
     edges[...] = packed
 
+    core_edges = total_edges // 2
+    first = core * core_edges
+
+    def gather(k, fresh):
+        for t in range(core_edges // TILE):
+            r_row = edges[1:2, pl.ds(pl.multiple_of(first + t * TILE, TILE), TILE)]
+            col = lax.broadcasted_iota(jnp.int32, (chunk, TILE), 0) + k * chunk
+            pick = jnp.where(col == r_row, 1.0, 0.0).astype(BF16)
+            found = dot(rbuf[k], pick)
+            at = slice(t * TILE, (t + 1) * TILE)
+            right_rows_s[:, at] = found if fresh else right_rows_s[:, at] + found
+
     passes = []
     for i in range(CHUNKS // 2):
         k = core * (CHUNKS // 2) + i
@@ -228,6 +239,7 @@
             )
         )
         passes[-1].start()
+        gather(k, i == 0)
     for i in range(CHUNKS // 2):
         k = (1 - core) * (CHUNKS // 2) + i
         pltpu.make_async_remote_copy(
@@ -238,20 +250,19 @@
             device_id=(b, sibling),
             device_id_type=MESH,
         ).wait_recv()
+        gather(k, False)
 
     rel_acc[...] = jnp.zeros_like(rel_acc)
     own_start = pl.multiple_of(s * own_width, own_width)
-
-    def tile_step(t, _):
-        at = pl.ds(pl.multiple_of(t * TILE, TILE), TILE)
-        l_row = edges[0:1, at]
-        r_row = edges[1:2, at]
-        t_row = edges[2:3, at]
-        right_rows = jnp.zeros((width, TILE), F32)
-        for k in range(CHUNKS):
-            col = lax.broadcasted_iota(jnp.int32, (chunk, TILE), 0) + k * chunk
-            pick = jnp.where(col == r_row, 1.0, 0.0).astype(BF16)
-            right_rows = right_rows + dot(rbuf[k], pick)
+    sib_start = pl.multiple_of(sibling * own_width, own_width)
+    chip_kind = (s - core) * (rel_count // n_span)
+
+    def tile_step(t):
+        at = slice(t * TILE, (t + 1) * TILE)
+        edge_at = pl.ds(pl.multiple_of(first + t * TILE, TILE), TILE)
+        l_row = edges[0:1, edge_at]
+        t_row = edges[2:3, edge_at]
+        right_rows = right_rows_s[:, at]
         kind = lax.broadcasted_iota(jnp.int32, (128, TILE), 0)
         pick_rel = jnp.where((kind & (rel_count - 1)) == t_row, 1.0, 0.0).astype(BF16)
         rot = dot(wcat[...], pick_rel)
@@ -268,10 +279,9 @@
         pos_weight = -1.0 / (1.0 + jnp.exp(positive))
         times = cnt[...]
         times = jnp.concatenate([times] * (TILE // 128), axis=1)
-        weight = times / (1.0 + jnp.exp(-scores))
+        weight = times * pl.reciprocal(1.0 + jnp.exp(-scores), approx=True)
         weight = (weight + jnp.where(is_left, pos_weight, 0.0)).astype(BF16)
-        w_tile[...] = weight
-        w_own[:, at] = w_tile[pl.ds(own_start, own_width), :]
+        w_s[:, at] = weight
         grad = dot(left[...], weight)
         a, c = grad[:half], grad[half:]
         rows = jnp.concatenate([a * w_re - c * w_im, a * w_im + c * w_re], axis=0)
@@ -279,12 +289,12 @@
         rrg_hi[:, at] = hi
         rrg_lo[:, at] = (rows - hi.astype(F32)).astype(BF16)
         turn = jnp.concatenate([a * r_re + c * r_im, a * r_im - c * r_re], axis=0).astype(BF16)
-        own_kind = lax.broadcasted_iota(jnp.int32, (16, TILE), 0) + s * (rel_count // n_span)
+        own_kind = lax.broadcasted_iota(jnp.int32, (16, TILE), 0) + chip_kind
         pick_own = jnp.where(own_kind == t_row, 1.0, 0.0).astype(BF16)
         rel_acc[...] += nt_dot(pick_own, turn)
-        return 0
-
-    lax.fori_loop(0, total_edges // TILE, tile_step, 0)
+
+    for t in range(core_edges // TILE):
+        tile_step(t)
 
     def exchange(buf, me, peers, slots_of, send_sem, recv_sem):
         copies = []
@@ -312,20 +322,48 @@
             copies[-1][0].start()
         return copies
 
+    def to_sibling(i, src, dst):
+        copy = pltpu.make_async_remote_copy(
+            src_ref=src,
+            dst_ref=dst,
+            send_sem=part_send.at[i],
+            recv_sem=part_recv.at[i],
+            device_id=(b, sibling),
+            device_id_type=MESH,
+        )
+        copy.start()
+        return copy
+
     rel_rows = rel_count // n_span
-    rb1[j] = rel_acc[0:rel_rows, :]
+    rel_part[0, 0] = rel_acc[0:rel_rows, :]
+    rel_part[0, 1] = rel_acc[rel_rows : 2 * rel_rows, :]
+    rel_half = to_sibling(0, rel_part.at[0, 1 - core], rel_part.at[1, 0])
+
+    r_own = edges[1:2, pl.ds(pl.multiple_of(first, core_edges), core_edges)]
+
+    def right_columns(start):
+        col = lax.broadcasted_iota(jnp.int32, (own_width, core_edges), 0) + start
+        pick = jnp.where(col == r_own, 1.0, 0.0).astype(BF16)
+        return nt_dot(rrg_hi[...], pick) + nt_dot(rrg_lo[...], pick)
+
+    def left_columns(start):
+        return nt_dot(query_s[...], w_s[pl.ds(start, own_width), :])
+
+    right_part[0] = right_columns(sib_start)
+    right_half = to_sibling(1, right_part.at[0], right_part.at[1])
+
+    rel_half.wait_recv()
+    rb1[j] = rel_part[0, core] + rel_part[1, 0]
     stage1 = exchange(
         rb1, j, inner_peers, [lax.rem(j + d, inner) for d in range(1, inner)], r1_send, r1_recv
     )
 
-    r_all = edges[1:2, :]
-    col = lax.broadcasted_iota(jnp.int32, (own_width, total_edges), 0) + s * own_width
-    pick = jnp.where(col == r_all, 1.0, 0.0).astype(BF16)
-    right_own = nt_dot(rrg_hi[...], pick) + nt_dot(rrg_lo[...], pick)
-    back_send[...] = right_own.astype(BF16)
+    right_own = right_columns(own_start)
+    right_half.wait_recv()
+    back_send[...] = (right_own + right_part[1]).astype(BF16)
     back = pltpu.make_async_remote_copy(
         src_ref=back_send,
-        dst_ref=back_recv,
+        dst_ref=right_out,
         send_sem=back_ssem,
         recv_sem=back_rsem,
         device_id=(prv, s),
@@ -333,6 +371,9 @@
     )
     back.start()
 
+    left_part[0] = left_columns(sib_start)
+    left_half = to_sibling(2, left_part.at[0], left_part.at[1])
+
     for _, incoming in stage1:
         incoming.wait_recv()
     rb2[zi] = jnp.sum(rb1[...], axis=0)
@@ -340,24 +381,45 @@
         rb2, zi, outer_peers, [lax.rem(zi + d, outer) for d in range(1, outer)], r2_send, r2_recv
     )
 
-    left_stage[...] = nt_dot(query_s[...], w_own[...])
+    left_own = left_columns(own_start)
+    left_half.wait_recv()
+    left_stage[...] = left_own + left_part[1]
     left_copy = pltpu.make_async_copy(left_stage, left_out, out_sem.at[0])
     left_copy.start()
 
     for _, incoming in stage2:
         incoming.wait_recv()
-    rb3[s] = jnp.sum(rb2[...], axis=0)
-    stage3 = exchange(
-        rb3, s, span_peers, [lax.rem(s + d, n_span) for d in range(1, n_span)], r3_send, r3_recv
-    )
+    rb3[...] = jnp.sum(rb2[...], axis=0)
+    own_rel = pltpu.make_async_copy(rb3, rel_out.at[s], out_sem.at[1])
+    own_rel.start()
+    stage3 = []
+    for d, (peer, other) in enumerate(
+        zip(span_peers, [lax.rem(s + d, n_span) for d in range(1, n_span)])
+    ):
+        stage3.append(
+            (
+                pltpu.make_async_remote_copy(
+                    src_ref=rb3,
+                    dst_ref=rel_out.at[s],
+                    send_sem=r3_send.at[d],
+                    recv_sem=r3_recv.at[s],
+                    device_id=peer,
+                    device_id_type=MESH,
+                ),
+                pltpu.make_async_remote_copy(
+                    src_ref=rb3,
+                    dst_ref=rel_out.at[other],
+                    send_sem=r3_send.at[d],
+                    recv_sem=r3_recv.at[other],
+                    device_id=peer,
+                    device_id_type=MESH,
+                ),
+            )
+        )
+        stage3[-1][0].start()
+    back.wait_recv()
     for _, incoming in stage3:
         incoming.wait_recv()
-    rel_copy = pltpu.make_async_copy(rb3, rel_out, out_sem.at[2])
-    rel_copy.start()
-
-    back.wait_recv()
-    right_copy = pltpu.make_async_copy(back_recv, right_out, out_sem.at[1])
-    right_copy.start()
 
     for copy in fwd + idx_copies + passes:
         copy.wait_send()
@@ -365,9 +427,35 @@
     for stage in (stage1, stage2, stage3):
         for outgoing, _ in stage:
             outgoing.wait_send()
+    for copy in (rel_half, right_half, left_half):
+        copy.wait_send()
     left_copy.wait()
+    own_rel.wait()
+
+
+def finish(left_in, right_in, rel_in, left_out, right_out, rel_out, left_v, right_b, right_f, rel_a, rel_b, sems):
+    groups, rows = rel_a.shape[0], rel_a.shape[1]
+    right_copy = pltpu.make_async_copy(right_in, right_b, sems.at[0])
+    right_copy.start()
+    rel_copy = pltpu.make_async_copy(rel_in, rel_a, sems.at[1])
+    rel_copy.start()
+    left_copy = pltpu.make_async_copy(left_in, left_v, sems.at[2])
+    left_copy.start()
+    right_copy.wait()
+    right_f[...] = right_b[...].astype(F32)
+    right_done = pltpu.make_async_copy(right_f, right_out, sems.at[3])
+    right_done.start()
+    left_copy.wait()
+    left_done = pltpu.make_async_copy(left_v, left_out, sems.at[5])
+    left_done.start()
     rel_copy.wait()
-    right_copy.wait()
+    for g in range(groups):
+        rel_b[g * rows : (g + 1) * rows, :] = rel_a[g]
+    rel_done = pltpu.make_async_copy(rel_b, rel_out, sems.at[4])
+    rel_done.start()
+    left_done.wait()
+    right_done.wait()
+    rel_done.wait()
 
 
 def solution(mesh):
@@ -401,12 +489,12 @@
                 jax.ShapeDtypeStruct((width, own), BF16),
                 jax.ShapeDtypeStruct((n_span, rel_rows, width), F32),
             ),
-            in_specs=[any_space] * 8,
+            in_specs=[pl.BlockSpec(memory_space=pltpu.HBM)] * 8,
             out_specs=[any_space] * 3,
             scratch_shapes=[
                 pltpu.VMEM((width, part), BF16),
                 pltpu.VMEM((part, width), BF16),
-                pltpu.VMEM((width, rel_count), F32),
+                pltpu.VMEM((rel_count, width), F32),
                 pltpu.VMEM((width, 128), BF16),
                 pltpu.VMEM((3, 1, slots), jnp.int32),
                 pltpu.VMEM((1, 1), jnp.int32),
@@ -415,18 +503,20 @@
                 pltpu.VMEM((n_span, 4, slots), jnp.int32),
                 pltpu.VMEM((4, total_edges), jnp.int32),
                 pltpu.VMEM((CHUNKS, width, part // CHUNKS), BF16),
-                pltpu.VMEM((width, total_edges), BF16),
-                pltpu.VMEM((part, TILE), BF16),
-                pltpu.VMEM((own, total_edges), BF16),
-                pltpu.VMEM((width, total_edges), BF16),
-                pltpu.VMEM((width, total_edges), BF16),
+                pltpu.VMEM((width, slots), BF16),
+                pltpu.VMEM((part, slots), BF16),
+                pltpu.VMEM((width, slots), BF16),
+                pltpu.VMEM((width, slots), BF16),
                 pltpu.VMEM((16, width), F32),
                 pltpu.VMEM((width, own), BF16),
-                pltpu.VMEM((width, own), BF16),
                 pltpu.VMEM((width, own), F32),
+                pltpu.VMEM((width, slots), F32),
+                pltpu.VMEM((2, 2, rel_rows, width), F32),
+                pltpu.VMEM((2, width, own), F32),
+                pltpu.VMEM((2, width, own), F32),
                 pltpu.VMEM((inner, rel_rows, width), F32),
                 pltpu.VMEM((outer, rel_rows, width), F32),
-                pltpu.VMEM((n_span, rel_rows, width), F32),
+                pltpu.VMEM((rel_rows, width), F32),
                 dma((7,)),
                 dma((n_span - 1,)),
                 dma((n_span,)),
@@ -435,29 +525,48 @@
                 dma((CHUNKS // 2,)),
                 dma,
                 dma,
+                dma((3,)),
+                dma((3,)),
                 dma((inner,)),
                 dma((inner,)),
                 dma((outer,)),
                 dma((outer,)),
                 dma((n_span,)),
                 dma((n_span,)),
-                dma((3,)),
+                dma((2,)),
             ],
             compiler_params=pltpu.CompilerParams(
-                collective_id=0, has_side_effects=True, vmem_limit_bytes=48 * 1024 * 1024
+                collective_id=0, has_side_effects=True, vmem_limit_bytes=63 * 1024 * 1024
             ),
         )(
             left_emb,
             right_emb,
-            relation_weight,
+            relation_weight.T,
             left_index,
             right_index,
             relation_index,
             edge_count,
             neg_index,
         )
-        rel_grad = rel_grad.reshape(rel_count, width).T
-        return left_grad, right_grad.astype(F32), rel_grad
+        left_grad, right_grad, rel_grad = pl.pallas_call(
+            finish,
+            out_shape=(
+                jax.ShapeDtypeStruct((width, own), F32),
+                jax.ShapeDtypeStruct((width, own), F32),
+                jax.ShapeDtypeStruct((rel_count, width), F32),
+            ),
+            in_specs=[any_space] * 3,
+            out_specs=[any_space] * 3,
+            scratch_shapes=[
+                pltpu.VMEM((width, own), F32),
+                pltpu.VMEM((width, own), BF16),
+                pltpu.VMEM((width, own), F32),
+                pltpu.VMEM((n_span, rel_rows, width), F32),
+                pltpu.VMEM((rel_count, width), F32),
+                dma((6,)),
+            ],
+        )(left_grad, right_grad, rel_grad)
+        return left_grad, right_grad, rel_grad.T
 
     in_specs = (
         P(None, "bucket"),

time: 62.7 us -> 48.5 us (0.77)
  Pallas kernels: 55.7 us -> 46.4 us
  local copies, waits for them, and re-layouts: 4.58 us -> 0 us
  other arithmetic: 0.78 us -> 0 us
    pallas_call x1, Pallas kernels: 55.7 us -> 44.4 us  [per_device(): pl.pallas_call(functools.partial(kernel, inner), out_shape=(jax.ShapeDtyp...]
    unnamed x14 -> x0, local copies, waits for them, and re-layouts: 3.95 us -> none
    pallas_call x0 -> x1, Pallas kernels: none -> 1.94 us  [per_device(): pl.pallas_call(finish, out_shape=(jax.ShapeDtypeStruct((width, own), F32)...]
    convert_element_type x1 -> x0, other arithmetic: 0.78 us -> none  [per_device(): return (left_grad, right_grad.astype(F32), rel_grad)]
    reshape x1 -> x0, local copies, waits for them, and re-layouts: 0.63 us -> none  [per_device(): rel_grad = rel_grad.reshape(rel_count, width).T]
where the time goes in v2:
time: 48.5 us; the launch traced here: 47.6 us
  Pallas kernels  46.4 us (96%)
  between operations  1.29 us (3%)
    pallas_call x1, Pallas kernels, per_device(): pl.pallas_call(functools.partial(kernel, inner), out_shape=(jax.ShapeDtyp...  44.4 us
    pallas_call x1, Pallas kernels, per_device(): pl.pallas_call(finish, out_shape=(jax.ShapeDtypeStruct((width, own), F32)...  1.94 us

profile of v2, /device:TPU:33, one launch (start us, length us, event | category | flops | bytes accessed | tf_op | source)
XLA Modules:
  0.0 47.6 jit_solution(14277198775079816032)
XLA Ops:
  1.3 44.4 %shard_map.103 = (f32[400,256]{1,0:T(8,128)}, bf16[400,256]{1,0:T(8,128)(2,1)}, f32[4,4,400]{2,1,0:T(4,128)}) custom-call(bf16[400,1024]{1,0:T(8,128)(2,1)} %left_hbm.1, bf16[400,1024]{1,0:T(8,128)(2,1)} %right_hbm.1, f32[16,400]{1,0:T(8,128)} %bitcast.2, s32[1,1,1024]{2,1,0:T(1,128)} %lidx_hbm.1, s32[1,1,1024]{2,1,0:T(1,128)} %ridx_hbm.1, ...), custom_call_target="tpu_custom_call" | custom-call | tf_op jit(solution)/shard_map/pallas_call | solution.py:485
  45.7 1.9 %shard_map.104 = (f32[400,256]{1,0:T(8,128)}, f32[400,256]{1,0:T(8,128)}, f32[16,400]{1,0:T(8,128)}) custom-call(f32[400,256]{1,0:T(8,128)} %get-tuple-element.9.left_in, bf16[400,256]{1,0:T(8,128)(2,1)} %get-tuple-element.10.right_in, f32[4,4,400]{2,1,0:T(4,128)} %get-tuple-element.11.rel_in), custom_call_target="tpu_custom_call" | custom-call | tf_op jit(solution)/shard_map/pallas_call | solution.py:551

commit v3 on v2

--- a/solution.py
+++ b/solution.py
@@ -75,8 +75,6 @@
     r1_recv,
     r2_send,
     r2_recv,
-    r3_send,
-    r3_recv,
     out_sem,
 ):
     width, part = left.shape
@@ -123,30 +121,7 @@
     for load in loads:
         load.start()
 
-    for load in loads[:4]:
-        load.wait()
-    slot = lax.broadcasted_iota(jnp.int32, (1, slots), 1)
-    live = slot < own_count[...]
-    idx_buf[s, 0:1, :] = jnp.where(live, own_idx[0], -1)
-    idx_buf[s, 1:2, :] = own_idx[1]
-    idx_buf[s, 2:3, :] = own_idx[2]
-    idx_buf[s, 3:4, :] = jnp.zeros((1, slots), jnp.int32)
-
     pl.semaphore_wait(barrier, len(peers))
-
-    idx_copies = []
-    for d, peer in enumerate(span_peers):
-        idx_copies.append(
-            pltpu.make_async_remote_copy(
-                src_ref=idx_buf.at[s],
-                dst_ref=idx_buf.at[s],
-                send_sem=idx_send.at[d],
-                recv_sem=idx_recv.at[s],
-                device_id=peer,
-                device_id_type=MESH,
-            )
-        )
-        idx_copies[-1].start()
 
     fwd = []
     for i in range(CHUNKS // 2):
@@ -162,6 +137,29 @@
             )
         )
         fwd[-1].start()
+
+    for load in loads[:4]:
+        load.wait()
+    slot = lax.broadcasted_iota(jnp.int32, (1, slots), 1)
+    live = slot < own_count[...]
+    idx_buf[s, 0:1, :] = jnp.where(live, own_idx[0], -1)
+    idx_buf[s, 1:2, :] = own_idx[1]
+    idx_buf[s, 2:3, :] = own_idx[2]
+    idx_buf[s, 3:4, :] = jnp.zeros((1, slots), jnp.int32)
+
+    idx_copies = []
+    for d, peer in enumerate(span_peers):
+        idx_copies.append(
+            pltpu.make_async_remote_copy(
+                src_ref=idx_buf.at[s],
+                dst_ref=idx_buf.at[s],
+                send_sem=idx_send.at[d],
+                recv_sem=idx_recv.at[s],
+                device_id=peer,
+                device_id_type=MESH,
+            )
+        )
+        idx_copies[-1].start()
 
     loads[4].wait()
     for k in range(part // 128):
@@ -255,7 +253,6 @@
     rel_acc[...] = jnp.zeros_like(rel_acc)
     own_start = pl.multiple_of(s * own_width, own_width)
     sib_start = pl.multiple_of(sibling * own_width, own_width)
-    chip_kind = (s - core) * (rel_count // n_span)
 
     def tile_step(t):
         at = slice(t * TILE, (t + 1) * TILE)
@@ -289,7 +286,7 @@
         rrg_hi[:, at] = hi
         rrg_lo[:, at] = (rows - hi.astype(F32)).astype(BF16)
         turn = jnp.concatenate([a * r_re + c * r_im, a * r_im - c * r_re], axis=0).astype(BF16)
-        own_kind = lax.broadcasted_iota(jnp.int32, (16, TILE), 0) + chip_kind
+        own_kind = lax.broadcasted_iota(jnp.int32, (rel_count, TILE), 0)
         pick_own = jnp.where(own_kind == t_row, 1.0, 0.0).astype(BF16)
         rel_acc[...] += nt_dot(pick_own, turn)
 
@@ -334,7 +331,7 @@
         copy.start()
         return copy
 
-    rel_rows = rel_count // n_span
+    rel_rows = rel_count // 2
     rel_part[0, 0] = rel_acc[0:rel_rows, :]
     rel_part[0, 1] = rel_acc[rel_rows : 2 * rel_rows, :]
     rel_half = to_sibling(0, rel_part.at[0, 1 - core], rel_part.at[1, 0])
@@ -390,54 +387,35 @@
     for _, incoming in stage2:
         incoming.wait_recv()
     rb3[...] = jnp.sum(rb2[...], axis=0)
-    own_rel = pltpu.make_async_copy(rb3, rel_out.at[s], out_sem.at[1])
+    own_rel = pltpu.make_async_copy(rb3, rel_out.at[core], out_sem.at[1])
     own_rel.start()
-    stage3 = []
-    for d, (peer, other) in enumerate(
-        zip(span_peers, [lax.rem(s + d, n_span) for d in range(1, n_span)])
-    ):
-        stage3.append(
-            (
-                pltpu.make_async_remote_copy(
-                    src_ref=rb3,
-                    dst_ref=rel_out.at[s],
-                    send_sem=r3_send.at[d],
-                    recv_sem=r3_recv.at[s],
-                    device_id=peer,
-                    device_id_type=MESH,
-                ),
-                pltpu.make_async_remote_copy(
-                    src_ref=rb3,
-                    dst_ref=rel_out.at[other],
-                    send_sem=r3_send.at[d],
-                    recv_sem=r3_recv.at[other],
-                    device_id=peer,
-                    device_id_type=MESH,
-                ),
-            )
-        )
-        stage3[-1][0].start()
+    rel_whole = to_sibling(3, rb3, rel_out.at[core])
     back.wait_recv()
-    for _, incoming in stage3:
-        incoming.wait_recv()
+    pltpu.make_async_remote_copy(
+        src_ref=rb3,
+        dst_ref=rel_out.at[1 - core],
+        send_sem=part_send.at[3],
+        recv_sem=part_recv.at[3],
+        device_id=(b, sibling),
+        device_id_type=MESH,
+    ).wait_recv()
 
     for copy in fwd + idx_copies + passes:
         copy.wait_send()
     back.wait_send()
-    for stage in (stage1, stage2, stage3):
+    for stage in (stage1, stage2):
         for outgoing, _ in stage:
             outgoing.wait_send()
-    for copy in (rel_half, right_half, left_half):
+    for copy in (rel_half, right_half, left_half, rel_whole):
         copy.wait_send()
     left_copy.wait()
     own_rel.wait()
 
 
-def finish(left_in, right_in, rel_in, left_out, right_out, rel_out, left_v, right_b, right_f, rel_a, rel_b, sems):
-    groups, rows = rel_a.shape[0], rel_a.shape[1]
+def finish(left_in, right_in, rel_in, left_out, right_out, rel_out, left_v, right_b, right_f, rel_v, sems):
     right_copy = pltpu.make_async_copy(right_in, right_b, sems.at[0])
     right_copy.start()
-    rel_copy = pltpu.make_async_copy(rel_in, rel_a, sems.at[1])
+    rel_copy = pltpu.make_async_copy(rel_in, rel_v, sems.at[1])
     rel_copy.start()
     left_copy = pltpu.make_async_copy(left_in, left_v, sems.at[2])
     left_copy.start()
@@ -449,9 +427,7 @@
     left_done = pltpu.make_async_copy(left_v, left_out, sems.at[5])
     left_done.start()
     rel_copy.wait()
-    for g in range(groups):
-        rel_b[g * rows : (g + 1) * rows, :] = rel_a[g]
-    rel_done = pltpu.make_async_copy(rel_b, rel_out, sems.at[4])
+    rel_done = pltpu.make_async_copy(rel_v, rel_out, sems.at[4])
     rel_done.start()
     left_done.wait()
     right_done.wait()
@@ -479,7 +455,7 @@
         total_edges = 2 * slots
         own = part // n_span
         rel_count = relation_weight.shape[1]
-        rel_rows = rel_count // n_span
+        rel_rows = rel_count // 2
         any_space = pl.BlockSpec(memory_space=pl.ANY)
         dma = pltpu.SemaphoreType.DMA
         left_grad, right_grad, rel_grad = pl.pallas_call(
@@ -487,7 +463,7 @@
             out_shape=(
                 jax.ShapeDtypeStruct((width, own), F32),
                 jax.ShapeDtypeStruct((width, own), BF16),
-                jax.ShapeDtypeStruct((n_span, rel_rows, width), F32),
+                jax.ShapeDtypeStruct((2, rel_rows, width), F32),
             ),
             in_specs=[pl.BlockSpec(memory_space=pltpu.HBM)] * 8,
             out_specs=[any_space] * 3,
@@ -507,7 +483,7 @@
                 pltpu.VMEM((part, slots), BF16),
                 pltpu.VMEM((width, slots), BF16),
                 pltpu.VMEM((width, slots), BF16),
-                pltpu.VMEM((16, width), F32),
+                pltpu.VMEM((rel_count, width), F32),
                 pltpu.VMEM((width, own), BF16),
                 pltpu.VMEM((width, own), F32),
                 pltpu.VMEM((width, slots), F32),
@@ -525,14 +501,12 @@
                 dma((CHUNKS // 2,)),
                 dma,
                 dma,
-                dma((3,)),
-                dma((3,)),
+                dma((4,)),
+                dma((4,)),
                 dma((inner,)),
                 dma((inner,)),
                 dma((outer,)),
                 dma((outer,)),
-                dma((n_span,)),
-                dma((n_span,)),
                 dma((2,)),
             ],
             compiler_params=pltpu.CompilerParams(
@@ -561,11 +535,10 @@
                 pltpu.VMEM((width, own), F32),
                 pltpu.VMEM((width, own), BF16),
                 pltpu.VMEM((width, own), F32),
-                pltpu.VMEM((n_span, rel_rows, width), F32),
                 pltpu.VMEM((rel_count, width), F32),
                 dma((6,)),
             ],
-        )(left_grad, right_grad, rel_grad)
+        )(left_grad, right_grad, rel_grad.reshape(rel_count, width))
         return left_grad, right_grad, rel_grad.T
 
     in_specs = (

time: 48.5 us -> 46.2 us (0.953); the launches traced: 47.6 us -> 46.1 us
  Pallas kernels: 46.4 us -> 44.8 us
    pallas_call x1, Pallas kernels: 44.4 us -> 42.8 us  [per_device(): pl.pallas_call(functools.partial(kernel, inner), out_shape=(jax.ShapeDtyp...]
where the time goes in v3:
time: 46.2 us; the launch traced here: 46.1 us
  Pallas kernels  44.8 us (97%)
  between operations  1.29 us (3%)
    pallas_call x1, Pallas kernels, per_device(): pl.pallas_call(functools.partial(kernel, inner), out_shape=(jax.ShapeDtyp...  42.8 us
    pallas_call x1, Pallas kernels, per_device(): pl.pallas_call(finish, out_shape=(jax.ShapeDtypeStruct((width, own), F32)...  1.94 us

profile of v3, /device:TPU:33, one launch (start us, length us, event | category | flops | bytes accessed | tf_op | source)
XLA Modules:
  0.0 46.1 jit_solution(2007566218986011821)
XLA Ops:
  1.3 42.8 %shard_map.103 = (f32[400,256]{1,0:T(8,128)}, bf16[400,256]{1,0:T(8,128)(2,1)}, f32[2,8,400]{2,1,0:T(8,128)}) custom-call(bf16[400,1024]{1,0:T(8,128)(2,1)} %left_hbm.1, bf16[400,1024]{1,0:T(8,128)(2,1)} %right_hbm.1, f32[16,400]{1,0:T(8,128)} %bitcast.3, s32[1,1,1024]{2,1,0:T(1,128)} %lidx_hbm.1, s32[1,1,1024]{2,1,0:T(1,128)} %ridx_hbm.1, ...), custom_call_target="tpu_custom_call" | custom-call | tf_op jit(solution)/shard_map/pallas_call | solution.py:461
  44.1 1.9 %shard_map.104 = (f32[400,256]{1,0:T(8,128)}, f32[400,256]{1,0:T(8,128)}, f32[16,400]{1,0:T(8,128)}) custom-call(f32[400,256]{1,0:T(8,128)} %get-tuple-element.9.left_in, bf16[400,256]{1,0:T(8,128)(2,1)} %get-tuple-element.10.right_in, f32[16,400]{1,0:T(8,128)} %bitcast.4), custom_call_target="tpu_custom_call" | custom-call | tf_op jit(solution)/shard_map/pallas_call | solution.py:525

commit v4 on v3

--- a/solution.py
+++ b/solution.py
@@ -55,6 +55,10 @@
     back_send,
     left_stage,
     right_rows_s,
+    left_rows_s,
+    rot_s,
+    grad_s,
+    pos_s,
     rel_part,
     right_part,
     left_part,
@@ -101,7 +105,7 @@
     span_peers = [(b, lax.rem(s + d, n_span)) for d in range(1, n_span)]
     inner_peers = [(zi * inner + lax.rem(j + d, inner), s) for d in range(1, inner)]
     outer_peers = [(lax.rem(zi + d, outer) * inner + j, s) for d in range(1, outer)]
-    peers = peers + span_peers + inner_peers + outer_peers
+    peers = outer_peers[::-1] + span_peers + inner_peers + peers
     for peer in peers:
         pl.semaphore_signal(barrier, inc=1, device_id=peer, device_id_type=MESH)
     loads = [
@@ -192,26 +196,45 @@
             device_id=(b, c),
             device_id_type=MESH,
         ).wait_recv()
-    rank = lax.broadcasted_iota(jnp.int32, (4, total_edges), 1)
-    packed = jnp.zeros((4, total_edges), jnp.int32)
-    start = jnp.zeros((1, 1), jnp.int32)
-    for c in range(n_span):
-        value = idx_buf[c]
-        alive = jnp.where(value[0:1, :] >= 0, 1.0, 0.0).astype(F32)
-        size = jnp.sum(alive, axis=1, keepdims=True).astype(jnp.int32)
-        value = jnp.concatenate([value, jnp.zeros((4, total_edges - slots), jnp.int32)], axis=1)
-        if c > 0:
-            for bit in range((total_edges - 1).bit_length()):
-                moved = pltpu.roll(value, 1 << bit, 1)
-                on = jnp.broadcast_to(start & (1 << bit), (4, total_edges)) != 0
-                value = jnp.where(on, moved, value)
-        inside = (rank >= start) & (rank < start + size)
-        packed = jnp.where(inside, value, packed)
-        start = start + size
-    edges[...] = packed
+    lefts = jnp.concatenate([idx_buf[c, 0:1, :] for c in range(n_span)], axis=0)
+    rights = jnp.concatenate([idx_buf[c, 1:2, :] for c in range(n_span)], axis=0)
+    kinds = jnp.concatenate([idx_buf[c, 2:3, :] for c in range(n_span)], axis=0)
+    sizes = jnp.sum(jnp.where(lefts >= 0, 1.0, 0.0).astype(F32), axis=1, keepdims=True)
+    sizes = sizes.astype(jnp.int32)
+    begins = [jnp.zeros((1, 1), jnp.int32)]
+    for c in range(n_span - 1):
+        begins.append(begins[-1] + sizes[c : c + 1])
+    start = jnp.concatenate(begins, axis=0)
+    bits = (part - 1).bit_length()
+    packed = jnp.maximum(lefts, 0) + (rights << bits) + (kinds << (2 * bits))
+    packed = jnp.concatenate(
+        [packed, jnp.zeros((n_span, total_edges - slots), jnp.int32)], axis=1
+    )
+    for bit in range((total_edges - 1).bit_length()):
+        moved = pltpu.roll(packed, 1 << bit, 1)
+        on = jnp.broadcast_to(start & (1 << bit), (n_span, total_edges)) != 0
+        packed = jnp.where(on, moved, packed)
+    rank = lax.broadcasted_iota(jnp.int32, (n_span, total_edges), 1)
+    packed = jnp.where((rank >= start) & (rank < start + sizes), packed, 0)
+    line = packed[0:1]
+    for c in range(1, n_span):
+        line = line + packed[c : c + 1]
+    edges[0:1, :] = line & (part - 1)
+    edges[1:2, :] = (line >> bits) & (part - 1)
+    edges[2:3, :] = line >> (2 * bits)
 
     core_edges = total_edges // 2
     first = core * core_edges
+
+    for t in range(core_edges // TILE):
+        at = slice(t * TILE, (t + 1) * TILE)
+        edge_at = pl.ds(pl.multiple_of(first + t * TILE, TILE), TILE)
+        kind = lax.broadcasted_iota(jnp.int32, (128, TILE), 0)
+        pick_rel = jnp.where((kind & (rel_count - 1)) == edges[2:3, edge_at], 1.0, 0.0).astype(BF16)
+        rot_s[:, at] = dot(wcat[...], pick_rel)
+        col = lax.broadcasted_iota(jnp.int32, (part, TILE), 0)
+        pick = jnp.where(col == edges[0:1, edge_at], 1.0, 0.0).astype(BF16)
+        left_rows_s[:, at] = dot(left[...], pick)
 
     def gather(k, fresh):
         for t in range(core_edges // TILE):
@@ -257,34 +280,26 @@
     def tile_step(t):
         at = slice(t * TILE, (t + 1) * TILE)
         edge_at = pl.ds(pl.multiple_of(first + t * TILE, TILE), TILE)
-        l_row = edges[0:1, edge_at]
         t_row = edges[2:3, edge_at]
         right_rows = right_rows_s[:, at]
-        kind = lax.broadcasted_iota(jnp.int32, (128, TILE), 0)
-        pick_rel = jnp.where((kind & (rel_count - 1)) == t_row, 1.0, 0.0).astype(BF16)
-        rot = dot(wcat[...], pick_rel)
+        left_rows = left_rows_s[:, at]
+        rot = rot_s[:, at]
         w_re, w_im = rot[:half], rot[half:]
         r_re, r_im = right_rows[:half], right_rows[half:]
         query = jnp.concatenate(
             [w_re * r_re + w_im * r_im, w_re * r_im - w_im * r_re], axis=0
         ).astype(BF16)
         query_s[:, at] = query
+        positive = jnp.sum(left_rows * query.astype(F32), axis=0, keepdims=True)
+        pos_weight = -1.0 / (1.0 + jnp.exp(positive))
+        pos_s[:, at] = pos_weight
         scores = dot(left_t[...], query)
-        col = lax.broadcasted_iota(jnp.int32, (part, TILE), 0)
-        is_left = col == l_row
-        positive = jnp.sum(jnp.where(is_left, scores, 0.0), axis=0, keepdims=True)
-        pos_weight = -1.0 / (1.0 + jnp.exp(positive))
-        times = cnt[...]
-        times = jnp.concatenate([times] * (TILE // 128), axis=1)
-        weight = times * pl.reciprocal(1.0 + jnp.exp(-scores), approx=True)
-        weight = (weight + jnp.where(is_left, pos_weight, 0.0)).astype(BF16)
+        times = jnp.concatenate([cnt[...]] * (TILE // 128), axis=1)
+        weight = (times * pl.reciprocal(1.0 + jnp.exp(-scores), approx=True)).astype(BF16)
         w_s[:, at] = weight
-        grad = dot(left[...], weight)
+        grad = dot(left[...], weight) + left_rows * pos_weight
+        grad_s[:, at] = grad
         a, c = grad[:half], grad[half:]
-        rows = jnp.concatenate([a * w_re - c * w_im, a * w_im + c * w_re], axis=0)
-        hi = rows.astype(BF16)
-        rrg_hi[:, at] = hi
-        rrg_lo[:, at] = (rows - hi.astype(F32)).astype(BF16)
         turn = jnp.concatenate([a * r_re + c * r_im, a * r_im - c * r_re], axis=0).astype(BF16)
         own_kind = lax.broadcasted_iota(jnp.int32, (rel_count, TILE), 0)
         pick_own = jnp.where(own_kind == t_row, 1.0, 0.0).astype(BF16)
@@ -336,6 +351,15 @@
     rel_part[0, 1] = rel_acc[rel_rows : 2 * rel_rows, :]
     rel_half = to_sibling(0, rel_part.at[0, 1 - core], rel_part.at[1, 0])
 
+    for t in range(core_edges // TILE):
+        at = slice(t * TILE, (t + 1) * TILE)
+        a, c = grad_s[:half, at], grad_s[half:, at]
+        w_re, w_im = rot_s[:half, at], rot_s[half:, at]
+        rows = jnp.concatenate([a * w_re - c * w_im, a * w_im + c * w_re], axis=0)
+        hi = rows.astype(BF16)
+        rrg_hi[:, at] = hi
+        rrg_lo[:, at] = (rows - hi.astype(F32)).astype(BF16)
+    l_own = edges[0:1, pl.ds(pl.multiple_of(first, core_edges), core_edges)]
     r_own = edges[1:2, pl.ds(pl.multiple_of(first, core_edges), core_edges)]
 
     def right_columns(start):
@@ -344,7 +368,13 @@
         return nt_dot(rrg_hi[...], pick) + nt_dot(rrg_lo[...], pick)
 
     def left_columns(start):
-        return nt_dot(query_s[...], w_s[pl.ds(start, own_width), :])
+        col = lax.broadcasted_iota(jnp.int32, (own_width, core_edges), 0) + start
+        pick = jnp.where(col == l_own, 1.0, 0.0).astype(BF16)
+        scaled = query_s[...].astype(F32) * pos_s[...]
+        hi = scaled.astype(BF16)
+        lo = (scaled - hi.astype(F32)).astype(BF16)
+        sums = nt_dot(query_s[...], w_s[pl.ds(start, own_width), :])
+        return sums + nt_dot(hi, pick) + nt_dot(lo, pick)
 
     right_part[0] = right_columns(sib_start)
     right_half = to_sibling(1, right_part.at[0], right_part.at[1])
@@ -477,7 +507,7 @@
                 pltpu.VMEM((1, neg_index.shape[1]), jnp.int32),
                 pltpu.VMEM((part, 128), F32),
                 pltpu.VMEM((n_span, 4, slots), jnp.int32),
-                pltpu.VMEM((4, total_edges), jnp.int32),
+                pltpu.VMEM((3, total_edges), jnp.int32),
                 pltpu.VMEM((CHUNKS, width, part // CHUNKS), BF16),
                 pltpu.VMEM((width, slots), BF16),
                 pltpu.VMEM((part, slots), BF16),
@@ -487,6 +517,10 @@
                 pltpu.VMEM((width, own), BF16),
                 pltpu.VMEM((width, own), F32),
                 pltpu.VMEM((width, slots), F32),
+                pltpu.VMEM((width, slots), F32),
+                pltpu.VMEM((width, slots), F32),
+                pltpu.VMEM((width, slots), F32),
+                pltpu.VMEM((1, slots), F32),
                 pltpu.VMEM((2, 2, rel_rows, width), F32),
                 pltpu.VMEM((2, width, own), F32),
                 pltpu.VMEM((2, width, own), F32),

time: 46.2 us -> 45.7 us (0.989)
  Pallas kernels: 44.8 us -> 44.3 us
    pallas_call x1, Pallas kernels: 42.8 us -> 42.4 us  [per_device(): pl.pallas_call(functools.partial(kernel, inner), out_shape=(jax.ShapeDtyp...]
where the time goes in v4:
time: 45.7 us; the launch traced here: 45.6 us
  Pallas kernels  44.3 us (97%)
  between operations  1.29 us (3%)
    pallas_call x1, Pallas kernels, per_device(): pl.pallas_call(functools.partial(kernel, inner), out_shape=(jax.ShapeDtyp...  42.4 us
    pallas_call x1, Pallas kernels, per_device(): pl.pallas_call(finish, out_shape=(jax.ShapeDtypeStruct((width, own), F32)...  1.94 us

profile of v4, /device:TPU:33, one launch (start us, length us, event | category | flops | bytes accessed | tf_op | source)
XLA Modules:
  0.0 45.6 jit_solution(17907219991705246136)
XLA Ops:
  1.3 42.4 %shard_map.103 = (f32[400,256]{1,0:T(8,128)}, bf16[400,256]{1,0:T(8,128)(2,1)}, f32[2,8,400]{2,1,0:T(8,128)}) custom-call(bf16[400,1024]{1,0:T(8,128)(2,1)} %left_hbm.1, bf16[400,1024]{1,0:T(8,128)(2,1)} %right_hbm.1, f32[16,400]{1,0:T(8,128)} %bitcast.3, s32[1,1,1024]{2,1,0:T(1,128)} %lidx_hbm.1, s32[1,1,1024]{2,1,0:T(1,128)} %ridx_hbm.1, ...), custom_call_target="tpu_custom_call" | custom-call | tf_op jit(solution)/shard_map/pallas_call | solution.py:491
  43.6 1.9 %shard_map.104 = (f32[400,256]{1,0:T(8,128)}, f32[400,256]{1,0:T(8,128)}, f32[16,400]{1,0:T(8,128)}) custom-call(f32[400,256]{1,0:T(8,128)} %get-tuple-element.9.left_in, bf16[400,256]{1,0:T(8,128)(2,1)} %get-tuple-element.10.right_in, f32[16,400]{1,0:T(8,128)} %bitcast.4), custom_call_target="tpu_custom_call" | custom-call | tf_op jit(solution)/shard_map/pallas_call | solution.py:559

commit v5 on v4

--- a/solution.py
+++ b/solution.py
@@ -50,7 +50,6 @@
     query_s,
     w_s,
     rrg_hi,
-    rrg_lo,
     rel_acc,
     back_send,
     left_stage,
@@ -356,16 +355,14 @@
         a, c = grad_s[:half, at], grad_s[half:, at]
         w_re, w_im = rot_s[:half, at], rot_s[half:, at]
         rows = jnp.concatenate([a * w_re - c * w_im, a * w_im + c * w_re], axis=0)
-        hi = rows.astype(BF16)
-        rrg_hi[:, at] = hi
-        rrg_lo[:, at] = (rows - hi.astype(F32)).astype(BF16)
+        rrg_hi[:, at] = rows.astype(BF16)
     l_own = edges[0:1, pl.ds(pl.multiple_of(first, core_edges), core_edges)]
     r_own = edges[1:2, pl.ds(pl.multiple_of(first, core_edges), core_edges)]
 
     def right_columns(start):
         col = lax.broadcasted_iota(jnp.int32, (own_width, core_edges), 0) + start
         pick = jnp.where(col == r_own, 1.0, 0.0).astype(BF16)
-        return nt_dot(rrg_hi[...], pick) + nt_dot(rrg_lo[...], pick)
+        return nt_dot(rrg_hi[...], pick)
 
     def left_columns(start):
         col = lax.broadcasted_iota(jnp.int32, (own_width, core_edges), 0) + start
@@ -403,7 +400,10 @@
 
     for _, incoming in stage1:
         incoming.wait_recv()
-    rb2[zi] = jnp.sum(rb1[...], axis=0)
+    plane = jnp.sum(rb1[...], axis=0)
+    blank = jnp.zeros((rel_rows, 512 - width), F32)
+    lower = jnp.concatenate([plane[:, 256:], blank], axis=1)
+    rb2[zi] = jnp.concatenate([plane[:, :256], lower], axis=0).astype(BF16)
     stage2 = exchange(
         rb2, zi, outer_peers, [lax.rem(zi + d, outer) for d in range(1, outer)], r2_send, r2_recv
     )
@@ -416,7 +416,9 @@
 
     for _, incoming in stage2:
         incoming.wait_recv()
-    rb3[...] = jnp.sum(rb2[...], axis=0)
+    whole = jnp.sum(rb2[...].astype(F32), axis=0)
+    rb3[:, :256] = whole[:rel_rows]
+    rb3[:, 256:] = whole[rel_rows:, : width - 256]
     own_rel = pltpu.make_async_copy(rb3, rel_out.at[core], out_sem.at[1])
     own_rel.start()
     rel_whole = to_sibling(3, rb3, rel_out.at[core])
@@ -512,7 +514,6 @@
                 pltpu.VMEM((width, slots), BF16),
                 pltpu.VMEM((part, slots), BF16),
                 pltpu.VMEM((width, slots), BF16),
-                pltpu.VMEM((width, slots), BF16),
                 pltpu.VMEM((rel_count, width), F32),
                 pltpu.VMEM((width, own), BF16),
                 pltpu.VMEM((width, own), F32),
@@ -525,7 +526,7 @@
                 pltpu.VMEM((2, width, own), F32),
                 pltpu.VMEM((2, width, own), F32),
                 pltpu.VMEM((inner, rel_rows, width), F32),
-                pltpu.VMEM((outer, rel_rows, width), F32),
+                pltpu.VMEM((outer, 2 * rel_rows, 256), BF16),
                 pltpu.VMEM((rel_rows, width), F32),
                 dma((7,)),
                 dma((n_span - 1,)),

time: 45.7 us -> 44.9 us (0.982)
  Pallas kernels: 44.3 us -> 43.5 us
    pallas_call x1, Pallas kernels: 42.4 us -> 41.6 us  [per_device(): pl.pallas_call(functools.partial(kernel, inner), out_shape=(jax.ShapeDtyp...]
where the time goes in v5:
time: 44.9 us; the launch traced here: 44.8 us
  Pallas kernels  43.5 us (97%)
  between operations  1.29 us (3%)
    pallas_call x1, Pallas kernels, per_device(): pl.pallas_call(functools.partial(kernel, inner), out_shape=(jax.ShapeDtyp...  41.6 us
    pallas_call x1, Pallas kernels, per_device(): pl.pallas_call(finish, out_shape=(jax.ShapeDtypeStruct((width, own), F32)...  1.94 us

profile of v5, /device:TPU:33, one launch (start us, length us, event | category | flops | bytes accessed | tf_op | source)
XLA Modules:
  0.0 44.8 jit_solution(17255068701492141313)
XLA Ops:
  1.3 41.6 %shard_map.103 = (f32[400,256]{1,0:T(8,128)}, bf16[400,256]{1,0:T(8,128)(2,1)}, f32[2,8,400]{2,1,0:T(8,128)}) custom-call(bf16[400,1024]{1,0:T(8,128)(2,1)} %left_hbm.1, bf16[400,1024]{1,0:T(8,128)(2,1)} %right_hbm.1, f32[16,400]{1,0:T(8,128)} %bitcast.3, s32[1,1,1024]{2,1,0:T(1,128)} %lidx_hbm.1, s32[1,1,1024]{2,1,0:T(1,128)} %ridx_hbm.1, ...), custom_call_target="tpu_custom_call" | custom-call | tf_op jit(solution)/shard_map/pallas_call | solution.py:493
  42.9 1.9 %shard_map.104 = (f32[400,256]{1,0:T(8,128)}, f32[400,256]{1,0:T(8,128)}, f32[16,400]{1,0:T(8,128)}) custom-call(f32[400,256]{1,0:T(8,128)} %get-tuple-element.9.left_in, bf16[400,256]{1,0:T(8,128)(2,1)} %get-tuple-element.10.right_in, f32[16,400]{1,0:T(8,128)} %bitcast.4), custom_call_target="tpu_custom_call" | custom-call | tf_op jit(solution)/shard_map/pallas_call | solution.py:560

commit v6 on v5

--- a/solution.py
+++ b/solution.py
@@ -377,7 +377,10 @@
     right_half = to_sibling(1, right_part.at[0], right_part.at[1])
 
     rel_half.wait_recv()
-    rb1[j] = rel_part[0, core] + rel_part[1, 0]
+    chip_sum = rel_part[0, core] + rel_part[1, 0]
+    blank = jnp.zeros((rel_rows, 512 - width), F32)
+    lower = jnp.concatenate([chip_sum[:, 256:], blank], axis=1)
+    rb1[j] = jnp.concatenate([chip_sum[:, :256], lower], axis=0).astype(BF16)
     stage1 = exchange(
         rb1, j, inner_peers, [lax.rem(j + d, inner) for d in range(1, inner)], r1_send, r1_recv
     )
@@ -400,10 +403,7 @@
 
     for _, incoming in stage1:
         incoming.wait_recv()
-    plane = jnp.sum(rb1[...], axis=0)
-    blank = jnp.zeros((rel_rows, 512 - width), F32)
-    lower = jnp.concatenate([plane[:, 256:], blank], axis=1)
-    rb2[zi] = jnp.concatenate([plane[:, :256], lower], axis=0).astype(BF16)
+    rb2[zi] = jnp.sum(rb1[...].astype(F32), axis=0).astype(BF16)
     stage2 = exchange(
         rb2, zi, outer_peers, [lax.rem(zi + d, outer) for d in range(1, outer)], r2_send, r2_recv
     )
@@ -525,7 +525,7 @@
                 pltpu.VMEM((2, 2, rel_rows, width), F32),
                 pltpu.VMEM((2, width, own), F32),
                 pltpu.VMEM((2, width, own), F32),
-                pltpu.VMEM((inner, rel_rows, width), F32),
+                pltpu.VMEM((inner, 2 * rel_rows, 256), BF16),
                 pltpu.VMEM((outer, 2 * rel_rows, 256), BF16),
                 pltpu.VMEM((rel_rows, width), F32),
                 dma((7,)),

time: 44.9 us -> 44.9 us (level)
  no operation moved by 1% of the time
where the time goes in v6:
time: 44.9 us; the launch traced here: 44.8 us
  Pallas kernels  43.5 us (97%)
  between operations  1.29 us (3%)
    pallas_call x1, Pallas kernels, per_device(): pl.pallas_call(functools.partial(kernel, inner), out_shape=(jax.ShapeDtyp...  41.6 us
    pallas_call x1, Pallas kernels, per_device(): pl.pallas_call(finish, out_shape=(jax.ShapeDtypeStruct((width, own), F32)...  1.94 us

profile of v6, /device:TPU:33, one launch (start us, length us, event | category | flops | bytes accessed | tf_op | source)
XLA Modules:
  0.0 44.8 jit_solution(3536336751727197558)
XLA Ops:
  1.3 41.6 %shard_map.103 = (f32[400,256]{1,0:T(8,128)}, bf16[400,256]{1,0:T(8,128)(2,1)}, f32[2,8,400]{2,1,0:T(8,128)}) custom-call(bf16[400,1024]{1,0:T(8,128)(2,1)} %left_hbm.1, bf16[400,1024]{1,0:T(8,128)(2,1)} %right_hbm.1, f32[16,400]{1,0:T(8,128)} %bitcast.3, s32[1,1,1024]{2,1,0:T(1,128)} %lidx_hbm.1, s32[1,1,1024]{2,1,0:T(1,128)} %ridx_hbm.1, ...), custom_call_target="tpu_custom_call" | custom-call | tf_op jit(solution)/shard_map/pallas_call | solution.py:493
  42.9 1.9 %shard_map.104 = (f32[400,256]{1,0:T(8,128)}, f32[400,256]{1,0:T(8,128)}, f32[16,400]{1,0:T(8,128)}) custom-call(f32[400,256]{1,0:T(8,128)} %get-tuple-element.9.left_in, bf16[400,256]{1,0:T(8,128)(2,1)} %get-tuple-element.10.right_in, f32[16,400]{1,0:T(8,128)} %bitcast.4), custom_call_target="tpu_custom_call" | custom-call | tf_op jit(solution)/shard_map/pallas_call | solution.py:560
